TPU v7x, 32 devices: a whole 2x2x4 slice. The times are simulated.
32 devices in a mesh: dp: 8 (over z, x), mp: 4 (over y, core).
Axes of the slice: x: 2, y: 2, z: 4, core: 2. Of those that a mesh axis runs over, the one named last changes fastest.
Arguments:
- tokens: bfloat16 [8, 2048, 1024], P('dp', 'mp'), may hold values from -6 to 6
- cotangent: bfloat16 [8, 2048, 1024], P('dp', 'mp'), may hold values from -6 to 6
- w_qkv: float32 [3, 1024, 1024], P(None, 'dp', 'mp'), may hold values from -0.1875 to 0.1875
- w_out: float32 [1024, 1024], P('mp', 'dp'), may hold values from -3 to 3
- w_up: float32 [1024, 4096], P('dp', 'mp'), may hold values from -0.1875 to 0.1875
- w_down: float32 [4096, 1024], P('mp', 'dp'), may hold values from -0.09375 to 0.09375
- gain_attn: float32 [1024], replicated, may hold values from 0.5 to 1.5
- shift_attn: float32 [1024], replicated, may hold values from -1.5 to 1.5
- gain_ffn: float32 [1024], replicated, may hold values from 0.5 to 1.5
- shift_ffn: float32 [1024], replicated, may hold values from -1.5 to 1.5
- bias_up: float32 [4096], P('mp'), may hold values from -1.5 to 1.5
- bias_down: float32 [1024], replicated, may hold values from -1.5 to 1.5
- random_blocks: int32 [8, 16, 30, 3], P('dp', 'mp'), may hold values from 1 to 30
Outputs:
- out_tokens: bfloat16 [8, 2048, 1024], P('dp', 'mp')
- grad_tokens: float32 [8, 2048, 1024], P('dp', 'mp')
- new_qkv: float32 [3, 1024, 1024], P(None, 'dp', 'mp')
- qkv_rows: float32 [3, 1024], P(None, 'dp')
- qkv_cols: float32 [3, 1024], P(None, 'mp')
- new_out: float32 [1024, 1024], P('mp', 'dp')
- out_rows: float32 [1024], P('mp')
- out_cols: float32 [1024], P('dp')
- new_up: float32 [1024, 4096], P('dp', 'mp')
- up_rows: float32 [1024], P('dp')
- up_cols: float32 [4096], P('mp')
- new_down: float32 [4096, 1024], P('mp', 'dp')
- down_rows: float32 [4096], P('mp')
- down_cols: float32 [1024], P('dp')
- grad_gain_attn: float32 [1024], replicated
- grad_shift_attn: float32 [1024], replicated
- grad_gain_ffn: float32 [1024], replicated
- grad_shift_ffn: float32 [1024], replicated
- grad_bias_up: float32 [4096], P('mp')
- grad_bias_down: float32 [1024], replicated
Inputs may be any that keep to these rules, and one draw needn't show every extreme that they name: `random_blocks`: every entry names a block of the same document other than its first and last; entries may repeat and may equal window blocks.
All inputs are finite; a program needn't handle non-finite values.
Results may differ from a plain program's by a relative error of at most 0.04.
Values may be sent and summed in bfloat16 or wider, within the bound.
No kernel may reach another device: no remote copies, remote signals or barrier semaphores. Data moves between devices by JAX's collectives and lax.ppermute only.
A program may use at most 192 MiB of HBM per device.

v0:
```python
import jax
import jax.numpy as jnp
from jax import lax
from jax.sharding import PartitionSpec as P

D = 1024
FF = 4096
BLOCK = 64


EPS_NORM = 1e-05
EPS_FACTOR = 1e-30
LEARN_RATE = 0.1
GELU_SCALE = 0.7978845608028654


def gelu_tanh(values):
    return (
        0.5 * values * (1.0 + jnp.tanh(GELU_SCALE * (values + 0.044715 * values * values * values)))
    )


def block_table(random_rows, blocks_all):
    middle = jnp.arange(1, blocks_all - 1, dtype=jnp.int32)[:, None]
    fixed = jnp.concatenate(
        [
            jnp.zeros_like(middle),
            middle - 1,
            middle,
            middle + 1,
            jnp.zeros_like(middle) + (blocks_all - 1),
        ],
        axis=1,
    )
    return jnp.concatenate([fixed, random_rows], axis=1)


def spread_rows(local_part):
    return lax.all_gather(local_part, "mp", axis=0, tiled=True)


def spread_grads(local_part):
    return lax.all_gather(local_part, "mp", axis=0, tiled=True)


def combine_heads(partial_value):
    return lax.psum_scatter(
        partial_value.astype(jnp.bfloat16), "mp", scatter_dimension=0, tiled=True
    ).astype(jnp.float32)


def combine_grads(partial_value):
    return lax.psum_scatter(
        partial_value.astype(jnp.bfloat16), "mp", scatter_dimension=0, tiled=True
    ).astype(jnp.float32)


def norm_forward(values, norm_gain, norm_shift):
    center = jnp.mean(values, axis=1, keepdims=True)
    spread = values - center
    variance = jnp.mean(spread * spread, axis=1, keepdims=True)
    inverse = lax.rsqrt(variance + EPS_NORM)
    normal = spread * inverse
    return ((normal * norm_gain + norm_shift).astype(jnp.bfloat16), normal, inverse)


def norm_backward(grad_norm, norm_gain, normal, inverse):
    scaled = grad_norm * norm_gain
    mean_plain = jnp.mean(scaled, axis=1, keepdims=True)
    mean_normal = jnp.mean(scaled * normal, axis=1, keepdims=True)
    grad_values = inverse * (scaled - mean_plain - normal * mean_normal)
    return (grad_values, jnp.sum(grad_norm * normal, axis=0), jnp.sum(grad_norm, axis=0))


def near_blocks(block_rows, key_table):
    return jnp.take(block_rows, key_table, axis=0).reshape(
        key_table.shape[0], -1, block_rows.shape[2]
    )


def attend_group(query_group, key_group, value_group, scaling):
    scores = (
        jnp.einsum("nqe,nke->nqk", query_group, key_group, preferred_element_type=jnp.float32)
        * scaling
    )
    highest = jnp.max(scores, axis=-1, keepdims=True)
    expanded = jnp.exp(scores - highest)
    summed = jnp.sum(expanded, axis=-1, keepdims=True)
    probs = (expanded / summed).astype(jnp.bfloat16)
    result = jnp.einsum("nqk,nke->nqe", probs, value_group, preferred_element_type=jnp.float32)
    return (result, highest + jnp.log(summed))


def attend_back(query_group, key_group, value_group, grad_group, log_total, scaling):
    scores = (
        jnp.einsum("nqe,nke->nqk", query_group, key_group, preferred_element_type=jnp.float32)
        * scaling
    )
    probs = jnp.exp(scores - log_total)
    grad_probs = jnp.einsum(
        "nqe,nke->nqk", grad_group, value_group, preferred_element_type=jnp.float32
    )
    center = jnp.sum(probs * grad_probs, axis=-1, keepdims=True)
    grad_score = (probs * (grad_probs - center)).astype(jnp.bfloat16)
    grad_query = (
        jnp.einsum("nqk,nke->nqe", grad_score, key_group, preferred_element_type=jnp.float32)
        * scaling
    )
    grad_key = (
        jnp.einsum("nqk,nqe->nke", grad_score, query_group, preferred_element_type=jnp.float32)
        * scaling
    )
    grad_value = jnp.einsum(
        "nqk,nqe->nke", probs.astype(jnp.bfloat16), grad_group, preferred_element_type=jnp.float32
    )
    return (grad_query, grad_key, grad_value)


def head_forward(queries, key_rows, value_rows, key_table):
    head_dim = queries.shape[1]
    blocks_all = queries.shape[0] // BLOCK
    scaling = head_dim ** (-0.5)
    query_blocks = queries.reshape(blocks_all, BLOCK, head_dim)
    key_near = near_blocks(key_rows.reshape(blocks_all, BLOCK, head_dim), key_table)
    value_near = near_blocks(value_rows.reshape(blocks_all, BLOCK, head_dim), key_table)
    out_mid, log_mid = attend_group(query_blocks[1:-1], key_near, value_near, scaling)
    query_ends = jnp.concatenate([query_blocks[0], query_blocks[-1]], axis=0)
    out_ends, log_ends = attend_group(query_ends[None], key_rows[None], value_rows[None], scaling)
    joined = jnp.concatenate([out_ends[:, :BLOCK], out_mid, out_ends[:, BLOCK:]], axis=0)
    return (joined.reshape(-1, head_dim).astype(jnp.bfloat16), log_mid, log_ends)


def head_backward(queries, key_rows, value_rows, key_table, grad_out, log_mid, log_ends):
    head_dim = queries.shape[1]
    blocks_all = queries.shape[0] // BLOCK
    scaling = head_dim ** (-0.5)
    query_blocks = queries.reshape(blocks_all, BLOCK, head_dim)
    grad_blocks = grad_out.reshape(blocks_all, BLOCK, head_dim)
    key_near = near_blocks(key_rows.reshape(blocks_all, BLOCK, head_dim), key_table)
    value_near = near_blocks(value_rows.reshape(blocks_all, BLOCK, head_dim), key_table)
    mid_query, mid_key, mid_value = attend_back(
        query_blocks[1:-1], key_near, value_near, grad_blocks[1:-1], log_mid, scaling
    )
    segment_ids = key_table.reshape(-1)
    key_sum = jax.ops.segment_sum(
        mid_key.reshape(-1, BLOCK, head_dim), segment_ids, num_segments=blocks_all
    ).reshape(-1, head_dim)
    value_sum = jax.ops.segment_sum(
        mid_value.reshape(-1, BLOCK, head_dim), segment_ids, num_segments=blocks_all
    ).reshape(-1, head_dim)
    query_ends = jnp.concatenate([query_blocks[0], query_blocks[-1]], axis=0)
    grad_ends = jnp.concatenate([grad_blocks[0], grad_blocks[-1]], axis=0)
    end_query, end_key, end_value = attend_back(
        query_ends[None], key_rows[None], value_rows[None], grad_ends[None], log_ends, scaling
    )
    grad_query = jnp.concatenate(
        [end_query[:, :BLOCK], mid_query, end_query[:, BLOCK:]], axis=0
    ).reshape(-1, head_dim)
    return (
        grad_query.astype(jnp.bfloat16),
        (key_sum + end_key[0]).astype(jnp.bfloat16),
        (value_sum + end_value[0]).astype(jnp.bfloat16),
    )


def factored(weight, gradient, row_sum, col_sum, whole_sum, row_total, col_total):
    row_mean = row_sum / col_total + EPS_FACTOR
    col_mean = col_sum / row_total + EPS_FACTOR
    whole = whole_sum / (row_total * col_total) + EPS_FACTOR
    row_factor = row_mean / whole[..., None]
    col_factor = col_mean / whole[..., None]
    update = gradient * lax.rsqrt(
        row_factor[..., :, None] * col_factor[..., None, :] * whole[..., None, None]
    )
    return (weight - LEARN_RATE * update, row_factor, col_factor)


def body(
    tokens,
    cotangent,
    w_qkv,
    w_out,
    w_up,
    w_down,
    gain_attn,
    shift_attn,
    gain_ffn,
    shift_ffn,
    bias_up,
    bias_down,
    random_blocks,
):
    qkv_low, out_low, up_low, down_low = (
        lax.all_gather(w_qkv.astype(jnp.bfloat16), "dp", axis=1, tiled=True),
        lax.all_gather(w_out.astype(jnp.bfloat16), "dp", axis=1, tiled=True),
        lax.all_gather(w_up.astype(jnp.bfloat16), "dp", axis=0, tiled=True),
        lax.all_gather(w_down.astype(jnp.bfloat16), "dp", axis=1, tiled=True),
    )
    local_heads = random_blocks.shape[1]
    head_dim = qkv_low.shape[2] // local_heads
    inputs = tokens[0].astype(jnp.float32)
    normed_low, normal_one, inverse_one = norm_forward(inputs, gain_attn, shift_attn)
    normed_full = spread_rows(normed_low)
    seq_rows = normed_full.shape[0]
    blocks_all = seq_rows // BLOCK
    tables = jax.vmap(lambda random_rows: block_table(random_rows, blocks_all))(random_blocks[0])
    project = jnp.einsum(
        "ld,cde->cle", normed_full, qkv_low, preferred_element_type=jnp.float32
    ).astype(jnp.bfloat16)
    heads_split = project.reshape(3, seq_rows, local_heads, head_dim).transpose(0, 2, 1, 3)
    attended, log_mid, log_ends = lax.map(
        lambda members: head_forward(*members),
        (heads_split[0], heads_split[1], heads_split[2], tables),
    )
    heads_out = attended.transpose(1, 0, 2).reshape(seq_rows, local_heads * head_dim)
    branch_part = jnp.dot(heads_out, out_low, preferred_element_type=jnp.float32)
    middle = inputs + combine_heads(branch_part)
    second_low, normal_two, inverse_two = norm_forward(middle, gain_ffn, shift_ffn)
    second_full = spread_rows(second_low)
    hidden_pre = jnp.dot(second_full, up_low, preferred_element_type=jnp.float32) + bias_up
    activated, gelu_pull = jax.vjp(gelu_tanh, hidden_pre)
    active_low = activated.astype(jnp.bfloat16)
    ffn_out = combine_heads(jnp.dot(active_low, down_low, preferred_element_type=jnp.float32))
    out_tokens = (middle + ffn_out + bias_down).astype(jnp.bfloat16)
    grad_top = cotangent[0]
    grad_top_full = spread_grads(grad_top)
    grad_down_w = jnp.einsum(
        "lf,ld->fd", active_low, grad_top_full, preferred_element_type=jnp.float32
    )
    grad_active = jnp.einsum(
        "ld,fd->lf", grad_top_full, down_low, preferred_element_type=jnp.float32
    )
    grad_hidden = gelu_pull(grad_active)[0].astype(jnp.bfloat16)
    grad_bias_up = jnp.sum(grad_hidden.astype(jnp.float32), axis=0)
    grad_up_w = jnp.einsum(
        "ld,lf->df", second_full, grad_hidden, preferred_element_type=jnp.float32
    )
    grad_second = combine_grads(
        jnp.einsum("lf,df->ld", grad_hidden, up_low, preferred_element_type=jnp.float32)
    )
    grad_middle_norm, grad_gain_ffn, grad_shift_ffn = norm_backward(
        grad_second, gain_ffn, normal_two, inverse_two
    )
    grad_top_float = grad_top.astype(jnp.float32)
    grad_middle = grad_top_float + grad_middle_norm
    grad_bias_down = jnp.sum(grad_top_float, axis=0)
    grad_branch_full = spread_grads(grad_middle.astype(jnp.bfloat16))
    grad_out_w = jnp.einsum(
        "la,ld->ad", heads_out, grad_branch_full, preferred_element_type=jnp.float32
    )
    grad_heads = jnp.einsum(
        "ld,ad->la", grad_branch_full, out_low, preferred_element_type=jnp.float32
    ).astype(jnp.bfloat16)
    grad_split = grad_heads.reshape(seq_rows, local_heads, head_dim).transpose(1, 0, 2)
    grad_query, grad_key, grad_value = lax.map(
        lambda members: head_backward(*members),
        (heads_split[0], heads_split[1], heads_split[2], tables, grad_split, log_mid, log_ends),
    )
    grad_project = (
        jnp.stack([grad_query, grad_key, grad_value])
        .transpose(0, 2, 1, 3)
        .reshape(3, seq_rows, local_heads * head_dim)
    )
    grad_qkv_w = jnp.einsum(
        "ld,cle->cde", normed_full, grad_project, preferred_element_type=jnp.float32
    )
    grad_normed = combine_grads(
        jnp.einsum("cle,cde->ld", grad_project, qkv_low, preferred_element_type=jnp.float32)
    )
    grad_input_norm, grad_gain_attn, grad_shift_attn = norm_backward(
        grad_normed, gain_attn, normal_one, inverse_one
    )
    grad_tokens = (grad_middle + grad_input_norm)[None]
    shard_qkv, shard_out, shard_up, shard_down = (
        lax.psum_scatter(
            grad_qkv_w.astype(jnp.bfloat16), "dp", scatter_dimension=1, tiled=True
        ).astype(jnp.float32),
        lax.psum_scatter(
            grad_out_w.astype(jnp.bfloat16), "dp", scatter_dimension=1, tiled=True
        ).astype(jnp.float32),
        lax.psum_scatter(
            grad_up_w.astype(jnp.bfloat16), "dp", scatter_dimension=0, tiled=True
        ).astype(jnp.float32),
        lax.psum_scatter(
            grad_down_w.astype(jnp.bfloat16), "dp", scatter_dimension=1, tiled=True
        ).astype(jnp.float32),
    )
    square_qkv = shard_qkv * shard_qkv
    square_out = shard_out * shard_out
    square_up = shard_up * shard_up
    square_down = shard_down * shard_down
    mp_terms = (
        jnp.sum(square_qkv, axis=2),
        jnp.sum(square_out, axis=0),
        jnp.sum(square_up, axis=1),
        jnp.sum(square_down, axis=0),
    )
    dp_terms = (
        jnp.sum(square_qkv, axis=1),
        jnp.sum(square_out, axis=1),
        jnp.sum(square_up, axis=0),
        jnp.sum(square_down, axis=1),
    )
    token_grads = (grad_gain_attn, grad_shift_attn, grad_gain_ffn, grad_shift_ffn, grad_bias_down)
    local_totals = (
        jnp.sum(square_qkv, axis=(1, 2)),
        jnp.sum(square_out),
        jnp.sum(square_up),
        jnp.sum(square_down),
    )
    mp_input = mp_terms + token_grads
    mp_sums = tuple(lax.psum(mp_input, "mp"))
    dp_input = dp_terms + mp_sums[4:9] + (grad_bias_up,)
    dp_sums = tuple(lax.psum(dp_input, "dp"))
    totals = tuple(
        lax.psum((local_totals[0], local_totals[1], local_totals[2], local_totals[3]), ("dp", "mp"))
    )
    new_qkv, qkv_rows, qkv_cols = factored(
        w_qkv, shard_qkv, mp_sums[0], dp_sums[0], totals[0], D, D
    )
    new_out, out_rows, out_cols = factored(
        w_out, shard_out, dp_sums[1], mp_sums[1], totals[1], D, D
    )
    new_up, up_rows, up_cols = factored(w_up, shard_up, mp_sums[2], dp_sums[2], totals[2], D, FF)
    new_down, down_rows, down_cols = factored(
        w_down, shard_down, dp_sums[3], mp_sums[3], totals[3], FF, D
    )
    return (
        out_tokens[None],
        grad_tokens,
        new_qkv,
        qkv_rows,
        qkv_cols,
        new_out,
        out_rows,
        out_cols,
        new_up,
        up_rows,
        up_cols,
        new_down,
        down_rows,
        down_cols,
        dp_sums[4],
        dp_sums[5],
        dp_sums[6],
        dp_sums[7],
        dp_sums[9],
        dp_sums[8],
    )


def solution(mesh):
    placed = (
        P("dp", "mp", None),
        P("dp", "mp", None),
        P(None, "dp", "mp"),
        P("mp", "dp"),
        P("dp", "mp"),
        P("mp", "dp"),
        P(),
        P(),
        P(),
        P(),
        P("mp"),
        P(),
        P("dp", "mp", None, None),
    )
    return jax.shard_map(
        body,
        mesh=mesh,
        in_specs=placed,
        out_specs=(
            P("dp", "mp", None),
            P("dp", "mp", None),
            P(None, "dp", "mp"),
            P(None, "dp"),
            P(None, "mp"),
            P("mp", "dp"),
            P("mp"),
            P("dp"),
            P("dp", "mp"),
            P("dp"),
            P("mp"),
            P("mp", "dp"),
            P("mp"),
            P("dp"),
            P(),
            P(),
            P(),
            P(),
            P("mp"),
            P(),
        ),
        check_vma=False,
    )
```

profile of v0, /device:TPU:0, one launch (start us, length us, event | category | flops | bytes accessed | tf_op | source)
XLA Modules:
  0.0 1205.1 jit_solution(2356265805523504589)
XLA Ops:
  15.6 31.7 %all_gather.26 = bf16[256,1024]{1,0:T(8,128)(2,1)S(1)} all-gather(bf16[256,128]{1,0:T(8,128)(2,1)S(1)} %convert_element_type.165), channel_id=1, replica_groups=mesh['dp'=8,'mp'=4] {'dp'}, dimensions={1}, use_global_device_ids=true | all-gather | bytes 589824 | tf_op jit(solution)/shard_map/all_gather | solution.py:195
  47.2 15.1 %all-gather.11.cloned.1.call-done = bf16[3,1024,256]{1,2,0:T(8,128)(2,1)} async-done(((bf16[3,128,256]{1,2,0:T(8,128)(2,1)}), bf16[3,1024,256]{1,2,0:T(8,128)(2,1)}) %all-gather.11.cloned.1.call-update) | async-done | bytes 1572880 | tf_op jit(solution)/shard_map/all_gather | solution.py:194
  62.3 35.4 %all-gather.9.cloned.1.call-done = bf16[2048,1024]{1,0:T(8,128)(2,1)} async-done(((bf16[512,1024]{1,0:T(8,128)(2,1)}), bf16[2048,1024]{1,0:T(8,128)(2,1)}) %all-gather.9.cloned.1.call-update) | async-done | bytes 4194320 | tf_op jit(solution)/shard_map/all_gather | solution.py:39
  97.8 7.8 fusion.54
  105.6 6.6 copy.98
  112.2 5.7 slice_bitcast_fusion
  119.0 85.0 %while.28 = (s32[]{:T(128)}, bf16[4,2048,64]{1,2,0:T(8,128)(2,1)}, f32[4,30,64,1]{2,1,3,0:T(8,128)}, f32[4,1,128,1]{2,3,1,0:T(1,128)}, bf16[4,2048,64]{2,1,0:T(8...) while((s32[]{:T(128)}, bf16[4,2048,64]{1,2,0:T(8,128)(2,1)}, ...), condition=%wide.region_7.9_spmd, body=%wide.region_2.8_spmd.sunk | while | flops 331841952 | bytes 38948568 | solution.py:211
  204.0 4.5 convolution_convert_fusion.1
  210.3 42.8 %reduce-scatter.15.cloned.1.call-done = bf16[512,1024]{1,0:T(8,128)(2,1)} async-done(((bf16[2048,1024]{1,0:T(8,128)(2,1)}), bf16[512,1024]{1,0:T(8,128)(2,1)}) %reduce-scatter.15.cloned.1.call-update) | async-done | bytes 1048592 | tf_op jit(solution)/shard_map/reduce_scatter | solution.py:47
  260.1 44.6 %all-gather.15.cloned.1.call-done = bf16[1024,1024]{1,0:T(8,128)(2,1)} async-done(((bf16[128,1024]{1,0:T(8,128)(2,1)}), bf16[1024,1024]{1,0:T(8,128)(2,1)}) %all-gather.15.cloned.1.call-update) | async-done | bytes 2097168 | tf_op jit(solution)/shard_map/all_gather | solution.py:196
  304.7 35.1 %all-gather.13.cloned.1.call-done = bf16[2048,1024]{1,0:T(8,128)(2,1)} async-done(((bf16[512,1024]{1,0:T(8,128)(2,1)}), bf16[2048,1024]{1,0:T(8,128)(2,1)}) %all-gather.13.cloned.1.call-update) | async-done | bytes 4194320 | tf_op jit(solution)/shard_map/all_gather | solution.py:39
  339.7 10.6 fusion.121
  350.4 43.2 %all-gather.17.cloned.1.call-done = bf16[1024,1024]{1,0:T(8,128)(2,1)} async-done(((bf16[1024,128]{1,0:T(8,128)(2,1)}), bf16[1024,1024]{1,0:T(8,128)(2,1)}) %all-gather.17.cloned.1.call-update) | async-done | bytes 2097168 | tf_op jit(solution)/shard_map/all_gather | solution.py:197
  393.5 34.3 %all-gather.21.cloned.1.call-done = bf16[1,2048,1024]{2,1,0:T(8,128)(2,1)} async-done(((bf16[1,512,1024]{2,1,0:T(8,128)(2,1)}), bf16[1,2048,1024]{2,1,0:T(8,128)(2,1)}) %all-gather.21.cloned.1.call-update) | async-done | bytes 4194320 | tf_op jit(solution)/shard_map/all_gather | solution.py:43
  427.9 15.6 %convert_reduce_fusion = (f32[1024]{0:T(1024)}, bf16[2048,1024]{1,0:T(8,128)(2,1)S(1)}) fusion(bf16[1024,1024]{1,0:T(8,128)(2,1)} %all-gather.17.cloned.1.call-done, bf16[1,2048,1024]{2,1,0:T(8,128)(2,1)} %all-gather.21.cloned.1.call-done, f32[2048,1024]{1,0:T(8,128)} %fusion.121, f32[1024]{0:T(1024)S(1)} %copy-done.59), kind=kOutput, calls=%fused_computation.108 | convolution fusion | flops 4351589376 | bytes 18882560 | tf_op jit(solution)/shard_map/ld,fd->lf/dot_general | solution.py:230
  445.5 6.3 convolution_convert_fusion.2
  452.0 44.4 %reduce-scatter.19.cloned.1.call-done = bf16[512,1024]{1,0:T(8,128)(2,1)} async-done(((bf16[2048,1024]{1,0:T(8,128)(2,1)}), bf16[512,1024]{1,0:T(8,128)(2,1)}) %reduce-scatter.19.cloned.1.call-update) | async-done | bytes 1048592 | tf_op jit(solution)/shard_map/reduce_scatter | solution.py:53
  503.9 10.6 fusion.85
  517.2 9.5 convolution_convert_fusion.5
  526.8 11.7 all-gather.19.cloned.1.call-done
  547.2 391.3 %while.29 = (s32[]{:T(128)}, bf16[4,2048,64]{1,2,0:T(8,128)(2,1)}, bf16[4,2048,64]{1,2,0:T(8,128)(2,1)}, bf16[4,2048,64]{1,2,0:T(8,128)(2,1)}, bf16[4,2048,64]{2...) while((s32[]{:T(128)}, bf16[4,2048,64]{1,2,0:T(8,128)(2,1)}, ...), condition=%wide.region_20.22_spmd, body=%wide.region_15.21_spmd.sunk | while | flops 817038464 | bytes 143667312 | solution.py:255
  563.1 3.9 broadcast_select_fusion.7
  580.8 4.8 fusion.220
  585.8 25.0 %scatter_fusion.1 = f32[32,64,64]{2,1,0:T(8,128)S(1)} fusion(f32[32,64,64]{2,1,0:T(8,128)S(1)} %broadcast.323.clone.1, s32[240]{0:T(256)S(1)} %copy-done.34, f32[240,64,64]{2,1,0:T(8,128)} %bitcast.349), kind=kCustom, calls=%fused_computation.5.clone.1 | custom fusion | flops 983040 | bytes 11797440 | tf_op jit(solution)/shard_map/while/body/eval_jaxpr/scatter-add | solution.py:148
  612.1 6.6 copy.154
  618.9 24.9 %scatter_fusion = f32[32,64,64]{2,1,0:T(8,128)S(1)} fusion(f32[32,64,64]{2,1,0:T(8,128)S(1)} %broadcast.323.clone, s32[240]{0:T(256)S(1)} %copy-done.34, f32[240,64,64]{2,1,0:T(8,128)} %bitcast.350), kind=kCustom, calls=%fused_computation.4.clone.1 | custom fusion | flops 983040 | bytes 11797440 | tf_op jit(solution)/shard_map/while/body/eval_jaxpr/scatter-add | solution.py:145
  678.7 4.8 fusion.220
  683.7 24.8 %scatter_fusion.1 = f32[32,64,64]{2,1,0:T(8,128)S(1)} fusion(f32[32,64,64]{2,1,0:T(8,128)S(1)} %broadcast.323.clone.1, s32[240]{0:T(256)S(1)} %copy-done.34, f32[240,64,64]{2,1,0:T(8,128)} %bitcast.349), kind=kCustom, calls=%fused_computation.5.clone.1 | custom fusion | flops 983040 | bytes 11797440 | tf_op jit(solution)/shard_map/while/body/eval_jaxpr/scatter-add | solution.py:148
  709.9 6.6 copy.154
  716.6 24.8 %scatter_fusion = f32[32,64,64]{2,1,0:T(8,128)S(1)} fusion(f32[32,64,64]{2,1,0:T(8,128)S(1)} %broadcast.323.clone, s32[240]{0:T(256)S(1)} %copy-done.34, f32[240,64,64]{2,1,0:T(8,128)} %bitcast.350), kind=kCustom, calls=%fused_computation.4.clone.1 | custom fusion | flops 983040 | bytes 11797440 | tf_op jit(solution)/shard_map/while/body/eval_jaxpr/scatter-add | solution.py:145
  776.4 4.8 fusion.220
  781.3 24.9 %scatter_fusion.1 = f32[32,64,64]{2,1,0:T(8,128)S(1)} fusion(f32[32,64,64]{2,1,0:T(8,128)S(1)} %broadcast.323.clone.1, s32[240]{0:T(256)S(1)} %copy-done.34, f32[240,64,64]{2,1,0:T(8,128)} %bitcast.349), kind=kCustom, calls=%fused_computation.5.clone.1 | custom fusion | flops 983040 | bytes 11797440 | tf_op jit(solution)/shard_map/while/body/eval_jaxpr/scatter-add | solution.py:148
  807.5 6.6 copy.154
  814.3 24.9 %scatter_fusion = f32[32,64,64]{2,1,0:T(8,128)S(1)} fusion(f32[32,64,64]{2,1,0:T(8,128)S(1)} %broadcast.323.clone, s32[240]{0:T(256)S(1)} %copy-done.34, f32[240,64,64]{2,1,0:T(8,128)} %bitcast.350), kind=kCustom, calls=%fused_computation.4.clone.1 | custom fusion | flops 983040 | bytes 11797440 | tf_op jit(solution)/shard_map/while/body/eval_jaxpr/scatter-add | solution.py:145
  874.0 4.8 fusion.220
  879.0 24.9 %scatter_fusion.1 = f32[32,64,64]{2,1,0:T(8,128)S(1)} fusion(f32[32,64,64]{2,1,0:T(8,128)S(1)} %broadcast.323.clone.1, s32[240]{0:T(256)S(1)} %copy-done.34, f32[240,64,64]{2,1,0:T(8,128)} %bitcast.349), kind=kCustom, calls=%fused_computation.5.clone.1 | custom fusion | flops 983040 | bytes 11797440 | tf_op jit(solution)/shard_map/while/body/eval_jaxpr/scatter-add | solution.py:148
  905.2 6.6 copy.154
  911.9 24.9 %scatter_fusion = f32[32,64,64]{2,1,0:T(8,128)S(1)} fusion(f32[32,64,64]{2,1,0:T(8,128)S(1)} %broadcast.323.clone, s32[240]{0:T(256)S(1)} %copy-done.34, f32[240,64,64]{2,1,0:T(8,128)} %bitcast.350), kind=kCustom, calls=%fused_computation.4.clone.1 | custom fusion | flops 983040 | bytes 11797440 | tf_op jit(solution)/shard_map/while/body/eval_jaxpr/scatter-add | solution.py:145
  938.5 4.7 convolution_convert_fusion.6
  948.7 4.5 fusion.92
  957.7 7.8 bitcast_convert_fusion
  967.1 11.1 convolution_convert_fusion.3
  984.0 23.3 %reduce-scatter.27.cloned.1.call-done = bf16[128,256]{1,0:T(8,128)(2,1)} async-done(((bf16[1024,256]{1,0:T(8,128)(2,1)}), bf16[128,256]{1,0:T(8,128)(2,1)}) %reduce-scatter.27.cloned.1.call-update) | async-done | bytes 65552
  1008.9 66.6 %reduce-scatter.25.cloned.1.call-done = bf16[128,768]{1,0:T(8,128)(2,1)} async-done(((bf16[1024,768]{1,0:T(8,128)(2,1)}), bf16[128,768]{1,0:T(8,128)(2,1)}) %reduce-scatter.25.cloned.1.call-update) | async-done | bytes 196624
  1080.8 40.4 %all-reduce = (f32[3]{0:T(128)}, f32[]{:T(128)}, f32[]{:T(128)}, f32[]{:T(128)}) all-reduce(f32[3]{0:T(128)} %get-tuple-element.246, f32[]{:T(128)} %get-tuple-element.249, f32[]{:T(128)} %get-tuple-element.243, f32[]{:T(128)} %get-tuple-element.240), channel_id=1, replica_groups=mesh['dp'=8,'mp'=4] {'dp','mp'}, use_global_device_ids=true, to_apply=%region_28.30 | all-reduce | flops 6 | bytes 48 | tf_op jit(solution)/shard_map/psum | solution.py:316
  1127.2 11.7 all-reduce.2
  1138.9 37.6 %all-reduce.1 = (f32[3,256]{1,0:T(4,128)}, f32[256]{0:T(256)}, f32[1024]{0:T(1024)}, f32[1024]{0:T(1024)}, f32[1024]{0:T(1024)}, /*index=5*/f32[1024]{0:T(1024)}...) all-reduce(f32[3,256]{1,0:T(4,128)} %get-tuple-element.247, ...), channel_id=1, replica_groups=mesh['dp'=8,'mp'=4] {'dp'}, use_global_device_ids=true, to_apply=%region_30.32 | all-reduce | flops 9216 | bytes 73728 | tf_op jit(solution)/shard_map/psum | solution.py:314
  1193.7 4.6 fusion.76
  (548 shorter events, 310.2 us)
Async XLA Ops:
  7.2 55.1 %all-gather.11.cloned.1.call-start = ((), (), s32[]{:S(2)}) async-start(), calls=%async_computation.9 | async-start | bytes 1769472 | tf_op jit(solution)/shard_map/all_gather | solution.py:194
  8.5 97.1 %copy-start.22 = (f32[3,128,256]{1,2,0:T(8,128)}, f32[3,128,256]{1,2,0:T(8,128)S(1)}, u32[]{:S(2)}) copy-start(f32[3,128,256]{1,2,0:T(8,128)S(1)} %copy.97) | copy-start | bytes 1179652
  9.3 88.5 %all-gather.9.cloned.1.call-start = ((), (), s32[]{:S(2)}) async-start(), calls=%async_computation.8 | async-start | bytes 5242880 | tf_op jit(solution)/shard_map/all_gather | solution.py:39
  14.6 238.5 %reduce-scatter.15.cloned.1.call-start = ((), (), s32[]{:S(2)}) async-start(), calls=%async_computation.10 | async-start | bytes 5242880 | tf_op jit(solution)/shard_map/reduce_scatter | solution.py:47
  47.2 156.7 %copy-start.26 = (bf16[256,1024]{1,0:T(8,128)(2,1)}, bf16[256,1024]{1,0:T(8,128)(2,1)S(1)}, u32[]{:S(2)}) copy-start(bf16[256,1024]{1,0:T(8,128)(2,1)S(1)} %all_gather.26) | copy-start | bytes 1572868
  208.4 48.1 %copy-start.37 = (f32[1024]{0:T(1024)S(1)}, f32[1024]{0:T(1024)}, u32[]{:S(2)}) copy-start(f32[1024]{0:T(1024)} %param.27) | copy-start | bytes 12292
  208.4 48.1 %copy-start.51 = (f32[1024]{0:T(1024)S(1)}, f32[1024]{0:T(1024)}, u32[]{:S(2)}) copy-start(f32[1024]{0:T(1024)} %param.28) | copy-start | bytes 12292
  208.5 96.2 %all-gather.15.cloned.1.call-start = ((), (), s32[]{:S(2)}) async-start(), calls=%async_computation.12 | async-start | bytes 2359296 | tf_op jit(solution)/shard_map/all_gather | solution.py:196
  210.2 47.9 %copy-start.28 = (f32[1024,128]{1,0:T(8,128)S(1)}, f32[1024,128]{1,0:T(8,128)}, u32[]{:S(2)}) copy-start(f32[1024,128]{1,0:T(8,128)} %param.24) | copy-start | bytes 1572868
  210.3 129.5 %all-gather.13.cloned.1.call-start = ((), (), s32[]{:S(2)}) async-start(), calls=%async_computation.11 | async-start | bytes 5242880 | tf_op jit(solution)/shard_map/all_gather | solution.py:39
  254.8 244.6 %copy-start.35 = (f32[512]{0:T(512)}, f32[512]{0:T(512)S(1)}, u32[]{:S(2)}) copy-start(f32[512]{0:T(512)S(1)} %broadcast_multiply_fusion.4) | copy-start | bytes 6148
  256.6 242.8 %copy-start.39 = (f32[512]{0:T(512)}, f32[512]{0:T(512)S(1)}, u32[]{:S(2)}) copy-start(f32[512]{0:T(512)S(1)} %add_rsqrt_fusion) | copy-start | bytes 6148
  258.1 135.4 %all-gather.17.cloned.1.call-start = ((), (), s32[]{:S(2)}) async-start(), calls=%async_computation.13 | async-start | bytes 2359296 | tf_op jit(solution)/shard_map/all_gather | solution.py:197
  258.9 168.9 %all-gather.21.cloned.1.call-start = ((), (), s32[]{:S(2)}) async-start(), calls=%async_computation.19 | async-start | bytes 5242880 | tf_op jit(solution)/shard_map/all_gather | solution.py:43
  259.7 168.2 %copy-start.59 = (f32[1024]{0:T(1024)S(1)}, f32[1024]{0:T(1024)}, u32[]{:S(2)}) copy-start(f32[1024]{0:T(1024)} %param.29) | copy-start | bytes 12292
  259.7 236.8 %reduce-scatter.19.cloned.1.call-start = ((), (), s32[]{:S(2)}) async-start(), calls=%async_computation.15 | async-start | bytes 5242880 | tf_op jit(solution)/shard_map/reduce_scatter | solution.py:53
  451.8 48.8 %copy-start.9 = (bf16[1,512,1024]{2,1,0:T(8,128)(2,1)S(1)}, bf16[1,512,1024]{2,1,0:T(8,128)(2,1)}, u32[]{:S(2)}) copy-start(bf16[1,512,1024]{2,1,0:T(8,128)(2,1)} %param.20) | copy-start | bytes 3145732
  451.8 86.7 %all-gather.19.cloned.1.call-start = ((), (), s32[]{:S(2)}) async-start(), calls=%async_computation.16 | async-start | bytes 5242880 | tf_op jit(solution)/shard_map/all_gather | solution.py:43
  503.8 476.4 %reduce-scatter.29.cloned.1.call-start = ((), (), s32[]{:S(2)}) async-start(), calls=%async_computation.22 | async-start | bytes 2359296
  517.1 465.1 %reduce-scatter.23.cloned.1.call-start = ((), (), s32[]{:S(2)}) async-start(), calls=%async_computation.18 | async-start | bytes 2359296 | tf_op jit(solution)/shard_map/reduce_scatter | solution.py:281
  526.7 480.5 %reduce-scatter.27.cloned.1.call-start = ((), (), s32[]{:S(2)}) async-start(), calls=%async_computation.21 | async-start | bytes 589824
  585.8 25.3 %copy-start.19 = (bf16[64,64]{1,0:T(8,128)(2,1)S(1)}, bf16[64,64]{1,0:T(8,128)(2,1)}, u32[]{:S(2)}) copy-start(bf16[64,64]{1,0:T(8,128)(2,1)} %copy-done.18) | copy-start | bytes 24580 | tf_op jit(solution)/shard_map/while
  585.8 25.3 %copy-start.21 = (bf16[64,64]{1,0:T(8,128)(2,1)S(1)}, bf16[64,64]{1,0:T(8,128)(2,1)}, u32[]{:S(2)}) copy-start(bf16[64,64]{1,0:T(8,128)(2,1)} %copy-done.20) | copy-start | bytes 24580 | tf_op jit(solution)/shard_map/while
  618.8 25.3 %copy-start.15 = (bf16[64,64]{1,0:T(8,128)(2,1)S(1)}, bf16[64,64]{1,0:T(8,128)(2,1)}, u32[]{:S(2)}) copy-start(bf16[64,64]{1,0:T(8,128)(2,1)} %copy-done.14) | copy-start | bytes 24580 | tf_op jit(solution)/shard_map/while
  618.8 25.3 %copy-start.17 = (bf16[64,64]{1,0:T(8,128)(2,1)S(1)}, bf16[64,64]{1,0:T(8,128)(2,1)}, u32[]{:S(2)}) copy-start(bf16[64,64]{1,0:T(8,128)(2,1)} %copy-done.16) | copy-start | bytes 24580 | tf_op jit(solution)/shard_map/while
  683.7 25.2 %copy-start.19 = (bf16[64,64]{1,0:T(8,128)(2,1)S(1)}, bf16[64,64]{1,0:T(8,128)(2,1)}, u32[]{:S(2)}) copy-start(bf16[64,64]{1,0:T(8,128)(2,1)} %copy-done.18) | copy-start | bytes 24580 | tf_op jit(solution)/shard_map/while
  683.7 25.2 %copy-start.21 = (bf16[64,64]{1,0:T(8,128)(2,1)S(1)}, bf16[64,64]{1,0:T(8,128)(2,1)}, u32[]{:S(2)}) copy-start(bf16[64,64]{1,0:T(8,128)(2,1)} %copy-done.20) | copy-start | bytes 24580 | tf_op jit(solution)/shard_map/while
  716.6 25.2 %copy-start.15 = (bf16[64,64]{1,0:T(8,128)(2,1)S(1)}, bf16[64,64]{1,0:T(8,128)(2,1)}, u32[]{:S(2)}) copy-start(bf16[64,64]{1,0:T(8,128)(2,1)} %copy-done.14) | copy-start | bytes 24580 | tf_op jit(solution)/shard_map/while
  781.3 25.2 %copy-start.19 = (bf16[64,64]{1,0:T(8,128)(2,1)S(1)}, bf16[64,64]{1,0:T(8,128)(2,1)}, u32[]{:S(2)}) copy-start(bf16[64,64]{1,0:T(8,128)(2,1)} %copy-done.18) | copy-start | bytes 24580 | tf_op jit(solution)/shard_map/while
  781.3 25.2 %copy-start.21 = (bf16[64,64]{1,0:T(8,128)(2,1)S(1)}, bf16[64,64]{1,0:T(8,128)(2,1)}, u32[]{:S(2)}) copy-start(bf16[64,64]{1,0:T(8,128)(2,1)} %copy-done.20) | copy-start | bytes 24580 | tf_op jit(solution)/shard_map/while
  814.2 25.2 %copy-start.15 = (bf16[64,64]{1,0:T(8,128)(2,1)S(1)}, bf16[64,64]{1,0:T(8,128)(2,1)}, u32[]{:S(2)}) copy-start(bf16[64,64]{1,0:T(8,128)(2,1)} %copy-done.14) | copy-start | bytes 24580 | tf_op jit(solution)/shard_map/while
  814.3 25.2 %copy-start.17 = (bf16[64,64]{1,0:T(8,128)(2,1)S(1)}, bf16[64,64]{1,0:T(8,128)(2,1)}, u32[]{:S(2)}) copy-start(bf16[64,64]{1,0:T(8,128)(2,1)} %copy-done.16) | copy-start | bytes 24580 | tf_op jit(solution)/shard_map/while
  879.0 25.2 %copy-start.19 = (bf16[64,64]{1,0:T(8,128)(2,1)S(1)}, bf16[64,64]{1,0:T(8,128)(2,1)}, u32[]{:S(2)}) copy-start(bf16[64,64]{1,0:T(8,128)(2,1)} %copy-done.18) | copy-start | bytes 24580 | tf_op jit(solution)/shard_map/while
  879.0 25.2 %copy-start.21 = (bf16[64,64]{1,0:T(8,128)(2,1)S(1)}, bf16[64,64]{1,0:T(8,128)(2,1)}, u32[]{:S(2)}) copy-start(bf16[64,64]{1,0:T(8,128)(2,1)} %copy-done.20) | copy-start | bytes 24580 | tf_op jit(solution)/shard_map/while
  911.9 25.2 %copy-start.15 = (bf16[64,64]{1,0:T(8,128)(2,1)S(1)}, bf16[64,64]{1,0:T(8,128)(2,1)}, u32[]{:S(2)}) copy-start(bf16[64,64]{1,0:T(8,128)(2,1)} %copy-done.14) | copy-start | bytes 24580 | tf_op jit(solution)/shard_map/while
  911.9 25.2 %copy-start.17 = (bf16[64,64]{1,0:T(8,128)(2,1)S(1)}, bf16[64,64]{1,0:T(8,128)(2,1)}, u32[]{:S(2)}) copy-start(bf16[64,64]{1,0:T(8,128)(2,1)} %copy-done.16) | copy-start | bytes 24580 | tf_op jit(solution)/shard_map/while
  945.3 130.1 %reduce-scatter.25.cloned.1.call-start = ((), (), s32[]{:S(2)}) async-start(), calls=%async_computation.20 | async-start | bytes 1769472
  957.7 166.7 %reduce-scatter.21.cloned.1.call-start = ((), (), s32[]{:S(2)}) async-start(), calls=%async_computation.17 | async-start | bytes 5242880 | tf_op jit(solution)/shard_map/reduce_scatter | solution.py:53
  965.5 228.1 %reduce-scatter.17.cloned.1.call-start = ((), (), s32[]{:S(2)}) async-start(), calls=%async_computation.14 | async-start | bytes 5242880 | tf_op jit(solution)/shard_map/reduce_scatter | solution.py:47
  978.2 146.1 %copy-start.6 = (bf16[1,512,1024]{2,1,0:T(8,128)(2,1)S(1)}, bf16[1,512,1024]{2,1,0:T(8,128)(2,1)}, u32[]{:S(2)}) copy-start(bf16[1,512,1024]{2,1,0:T(8,128)(2,1)} %param.19) | copy-start | bytes 3145732
  978.2 146.1 %copy-start.42 = (f32[512]{0:T(512)S(1)}, f32[512]{0:T(512)}, u32[]{:S(2)}) copy-start(f32[512]{0:T(512)} %copy-done.41) | copy-start | bytes 6148
  978.2 200.4 %copy-start.23 = (f32[3,128,256]{1,2,0:T(8,128)S(1)}, f32[3,128,256]{1,2,0:T(8,128)}, u32[]{:S(2)}) copy-start(f32[3,128,256]{1,2,0:T(8,128)} %copy-done.22) | copy-start | bytes 1179652
  981.3 94.1 %copy-start.25 = (bf16[1024,128]{1,0:T(8,128)(2,1)}, bf16[1024,128]{1,0:T(8,128)(2,1)S(1)}, u32[]{:S(2)}) copy-start(bf16[1024,128]{1,0:T(8,128)(2,1)S(1)} %copy.129) | copy-start | bytes 786436
  1008.2 67.2 %copy-start.32 = (bf16[256,128]{1,0:T(8,128)(2,1)}, bf16[256,128]{1,0:T(8,128)(2,1)S(1)}, u32[]{:S(2)}) copy-start(bf16[256,128]{1,0:T(8,128)(2,1)S(1)} %copy.127) | copy-start | bytes 196612
  1077.1 116.5 %copy-start.8 = (bf16[512,1024]{1,0:T(8,128)(2,1)S(1)}, bf16[512,1024]{1,0:T(8,128)(2,1)}, u32[]{:S(2)}) copy-start(bf16[512,1024]{1,0:T(8,128)(2,1)} %reduce-scatter.15.cloned.1.call-done) | copy-start | bytes 3145732
  1077.1 116.5 %copy-start.36 = (f32[512]{0:T(512)S(1)}, f32[512]{0:T(512)}, u32[]{:S(2)}) copy-start(f32[512]{0:T(512)} %copy-done.35) | copy-start | bytes 6148
  1077.1 116.5 %copy-start.38 = (f32[1024]{0:T(1024)S(1)}, f32[1024]{0:T(1024)}, u32[]{:S(2)}) copy-start(f32[1024]{0:T(1024)} %param.27) | copy-start | bytes 12292
  1077.2 116.5 %copy-start.40 = (f32[512]{0:T(512)S(1)}, f32[512]{0:T(512)}, u32[]{:S(2)}) copy-start(f32[512]{0:T(512)} %copy-done.39) | copy-start | bytes 6148
  (77 other events, 435.5 us)
Sparse Core Ops, SparseCore 0:
  10.7 51.6 all-gather.10
  64.5 33.2 all-gather.8
  208.6 44.5 reduce-scatter.14
  255.3 49.2 all-gather.14
  306.7 32.9 all-gather.12
  342.4 51.0 all-gather.16
  395.1 32.6 all-gather.20
  451.9 44.4 reduce-scatter.18
  504.0 34.4 all-gather.18
  541.9 67.8 reduce-scatter.28
  613.3 66.5 reduce-scatter.22
  945.4 61.7 reduce-scatter.26
  1011.6 63.7 reduce-scatter.24
  1077.8 44.0 reduce-scatter.20
  1124.4 44.6 reduce-scatter.16
where the time goes:
time: 1220 us; the launch traced here: 1210 us
  waiting for transfers between devices  397 us (33%)
  other arithmetic  303 us (25%)
  local copies, waits for them, and re-layouts  189 us (15%)
  matrix products  175 us (14%)
  blocking collectives  121 us (10%)
  between operations  16.6 us (1%)
    scatter-add x4, other arithmetic, head_backward(): jax.ops.segment_sum(mid_value.reshape(-1, BLOCK, head_dim), segment_ids,...  99.6 us
    scatter-add x4, other arithmetic, head_backward(): jax.ops.segment_sum(mid_key.reshape(-1, BLOCK, head_dim), segment_ids, nu...  99.5 us
    unnamed x18, waiting for transfers between devices  90.8 us
    all_gather x2, waiting for transfers between devices, spread_rows(): return lax.all_gather(local_part, 'mp', axis=0, tiled=True)  70.5 us
    gather x16, local copies, waits for them, and re-layouts, near_blocks(): jnp.take(block_rows, key_table, axis=0)  47.5 us
    all_gather x2, waiting for transfers between devices, spread_grads(): return lax.all_gather(local_part, 'mp', axis=0, tiled=True)  46 us
    all_gather x1, waiting for transfers between devices, body(): lax.all_gather(w_up.astype(jnp.bfloat16), 'dp', axis=0, tiled=True)  44.6 us
    reduce_scatter x2, waiting for transfers between devices, combine_grads(): lax.psum_scatter(partial_value.astype(jnp.bfloat16), 'mp', scatter_dimens...  44.4 us
  transfers between devices with their start and end apart: 15, of which 11 were waited for; matrix products, arithmetic and copies ran while one was open for 42% of the time, Pallas kernels for 0%

commit v1 on v0

v1 whole, which is shorter than its diff:
```python
import functools

import jax
import jax.numpy as jnp
from jax import lax
from jax.experimental import pallas as pl
from jax.experimental.pallas import tpu as pltpu
from jax.sharding import PartitionSpec as P

BLOCK = 64
EPS_NORM = 1e-05
EPS_FACTOR = 1e-30
LEARN_RATE = 0.1
GELU_SCALE = 0.7978845608028654
GELU_CUBE = 0.044715
F32 = jnp.float32
BF16 = jnp.bfloat16
NN = (((1,), (0,)), ((), ()))
NT = (((1,), (1,)), ((), ()))
TN = (((0,), (0,)), ((), ()))
VMEM_LIMIT = 40 << 20
CHUNKS = 1


def dot(left, right, form):
    return lax.dot_general(left, right, form, preferred_element_type=F32)


def swap(value, bit, size, axis="mp"):
    return lax.ppermute(value, axis, [(i, i ^ bit) for i in range(size)])


def gather_pieces(piece, size):
    if size != 4:
        whole = lax.all_gather(piece, "mp", axis=0, tiled=True)
        return [whole]
    near = swap(piece, 1, size)
    far = swap(piece, 2, size)
    return [piece, near, far, swap(far, 1, size)]


def scatter_sum(partial, size):
    low = partial.astype(BF16)
    rows = low.shape[0] // size
    if size != 4:
        return lax.psum_scatter(low, "mp", scatter_dimension=0, tiled=True).astype(F32)
    part = [low[n * rows : (n + 1) * rows] for n in range(4)]
    got = swap(jnp.concatenate([part[1], part[3]], axis=0), 1, size)
    own = partial[:rows] + got[:rows].astype(F32)
    other = (partial[2 * rows : 3 * rows] + got[rows:].astype(F32)).astype(BF16)
    return own + swap(other, 2, size).astype(F32)


def butterfly(value, axis, size):
    bit = 1
    while bit < size:
        value = value + swap(value, bit, size, axis)
        bit *= 2
    return value


def stack_heads(block, heads, head_dim):
    if heads == 1:
        return block
    owner = lax.broadcasted_iota(jnp.int32, block.shape, 1) // head_dim
    zero = jnp.zeros_like(block)
    return jnp.concatenate([jnp.where(owner == h, block, zero) for h in range(heads)], axis=0)


def unstack_heads(stacked, heads, head_dim):
    if heads == 1:
        return stacked
    rows = stacked.shape[0] // heads
    owner = lax.broadcasted_iota(jnp.int32, (rows, stacked.shape[1]), 1) // head_dim
    result = stacked[:rows]
    for h in range(1, heads):
        result = jnp.where(owner >= h, stacked[h * rows : (h + 1) * rows], result)
    return result


def block_rows(place):
    return pl.ds(pl.multiple_of(place * BLOCK, BLOCK), BLOCK)


def near_rows(ref, fixed, drawn, heads, head_dim):
    parts = [ref[block_rows(place), :] for place in fixed]
    for places in drawn:
        block = ref[block_rows(places[0]), :]
        if heads > 1:
            owner = lax.broadcasted_iota(jnp.int32, block.shape, 1) // head_dim
            for h in range(1, heads):
                block = jnp.where(owner >= h, ref[block_rows(places[h]), :], block)
        parts.append(block)
    return jnp.concatenate(parts, axis=0)


def probabilities(keys, queries):
    scores = dot(keys, queries, NT)
    expanded = jnp.exp(scores - jnp.max(scores, axis=0, keepdims=True))
    return expanded * (1.0 / jnp.sum(expanded, axis=0, keepdims=True))


def scale_low(block, scaling):
    return (block.astype(F32) * scaling).astype(BF16)


def table_of(random_ref, place, step, heads, draws):
    group = pl.program_id(0)
    fixed = [place(0), place(step), place(step + 1), place(step + 2), place(-1)]
    drawn = [
        [place(random_ref[group * heads + h, step * draws + j]) for h in range(heads)]
        for j in range(draws)
    ]
    return fixed, drawn


def placer(index_ref, blocks_all, pieces):
    per_piece = blocks_all // pieces

    def place(block):
        if isinstance(block, int):
            block = jnp.int32(block % blocks_all)
        if pieces == 1:
            return block
        return ((block // per_piece) ^ index_ref[0]) * per_piece + block % per_piece

    return place


def forward_kernel(heads, head_dim, draws, pieces, unroll, random_ref, index_ref, q_ref, k_ref, v_ref, o_ref):
    blocks_all = q_ref.shape[0] // BLOCK
    scaling = head_dim**-0.5
    place = placer(index_ref, blocks_all, pieces)

    def attend(queries, keys, values):
        stacked = stack_heads(scale_low(queries, scaling), heads, head_dim)
        probs = probabilities(keys, stacked).astype(BF16)
        return unstack_heads(dot(probs, values, TN), heads, head_dim).astype(BF16)

    def middle(step, carry):
        fixed, drawn = table_of(random_ref, place, step, heads, draws)
        keys = near_rows(k_ref, fixed, drawn, heads, head_dim)
        values = near_rows(v_ref, fixed, drawn, heads, head_dim)
        at = block_rows(fixed[2])
        o_ref[at, :] = attend(q_ref[at, :], keys, values)
        return carry

    lax.fori_loop(0, blocks_all - 2, middle, 0, unroll=unroll)
    for end in (0, -1):
        at = block_rows(place(end))
        o_ref[at, :] = attend(q_ref[at, :], k_ref[...], v_ref[...])


def backward_kernel(
    heads,
    head_dim,
    draws,
    pieces,
    unroll,
    random_ref,
    index_ref,
    q_ref,
    k_ref,
    v_ref,
    g_ref,
    dq_ref,
    dk_ref,
    dv_ref,
    k_near,
    v_near,
    k_drawn,
    v_drawn,
    k_ends,
    v_ends,
):
    blocks_all = q_ref.shape[0] // BLOCK
    scaling = head_dim**-0.5
    place = placer(index_ref, blocks_all, pieces)
    owner = lax.broadcasted_iota(jnp.int32, (BLOCK, q_ref.shape[1]), 1) // head_dim
    for ref in (k_drawn, v_drawn, k_ends, v_ends):
        ref[...] = jnp.zeros_like(ref)

    def back(queries, grads, keys, values):
        q_stack = stack_heads(scale_low(queries, scaling), heads, head_dim)
        g_stack = stack_heads(grads, heads, head_dim)
        probs = probabilities(keys, q_stack)
        grad_probs = dot(values, g_stack, NT)
        center = jnp.sum(probs * grad_probs, axis=0, keepdims=True)
        grad_scores = (probs * (grad_probs - center)).astype(BF16)
        grad_keys = dot(grad_scores, q_stack, NN)
        grad_values = dot(probs.astype(BF16), g_stack, NN)
        grad_queries = unstack_heads(dot(grad_scores, keys, TN), heads, head_dim) * scaling
        return grad_queries.astype(BF16), grad_keys, grad_values

    for number, end in enumerate((0, -1)):
        at = block_rows(place(end))
        dq, dk, dv = back(q_ref[at, :], g_ref[at, :], k_ref[...], v_ref[...])
        dq_ref[at, :] = dq
        if number == 0:
            k_near[...] = dk
            v_near[...] = dv
        else:
            k_near[...] += dk
            v_near[...] += dv

    def middle(step, carry):
        fixed, drawn = table_of(random_ref, place, step, heads, draws)
        keys = near_rows(k_ref, fixed, drawn, heads, head_dim)
        values = near_rows(v_ref, fixed, drawn, heads, head_dim)
        at = block_rows(fixed[2])
        dq, dk, dv = back(q_ref[at, :], g_ref[at, :], keys, values)
        dq_ref[at, :] = dq
        for part, near, far, ends in ((dk, k_near, k_drawn, k_ends), (dv, v_near, v_drawn, v_ends)):
            ends[0:BLOCK, :] += part[0:BLOCK]
            ends[BLOCK:, :] += part[4 * BLOCK : 5 * BLOCK]
            if pieces == 1:
                window = pl.ds(pl.multiple_of(step * BLOCK, BLOCK), 3 * BLOCK)
                near[window, :] += part[BLOCK : 4 * BLOCK]
            else:
                for n in range(1, 4):
                    near[block_rows(fixed[n]), :] += part[n * BLOCK : (n + 1) * BLOCK]
            for j in range(draws):
                block = part[(5 + j) * BLOCK : (6 + j) * BLOCK]
                for h in range(heads):
                    kept = block if heads == 1 else jnp.where(owner == h, block, 0.0)
                    far[block_rows(drawn[j][h]), :] += kept
        return carry

    lax.fori_loop(0, blocks_all - 2, middle, 0, unroll=unroll)
    for near, far, ends, out in ((k_near, k_drawn, k_ends, dk_ref), (v_near, v_drawn, v_ends, dv_ref)):
        near[block_rows(place(0)), :] += ends[0:BLOCK, :]
        near[block_rows(place(-1)), :] += ends[BLOCK:, :]
        out[...] = (near[...] + far[...]).astype(BF16)


def attention_call(kernel, unroll, project, grads, random_rows, index, pieces):
    seq_rows = project.shape[0]
    columns = project.shape[1] // 3
    local_heads, _, draws = random_rows.shape
    head_dim = columns // local_heads
    width = min(128, columns)
    groups = columns // width

    narrow = width < 128
    if narrow:
        operands = [project[:, n * columns : (n + 1) * columns] for n in range(3)]
    else:
        operands = [project] * 3

    def spec(part):
        first = 0 if narrow else part * groups
        return pl.BlockSpec((seq_rows, width), lambda g, *refs: (0, first + g))

    result = jax.ShapeDtypeStruct((seq_rows, columns), BF16)
    backward = grads is not None
    total = pltpu.VMEM((seq_rows, width), F32)
    ends = pltpu.VMEM((2 * BLOCK, width), F32)
    return pl.pallas_call(
        functools.partial(kernel, width // head_dim, head_dim, draws, pieces, unroll),
        grid_spec=pltpu.PrefetchScalarGridSpec(
            num_scalar_prefetch=2,
            grid=(groups,),
            in_specs=[spec(0), spec(1), spec(2)] + [spec(0)] * backward,
            out_specs=[spec(0)] * (3 if backward else 1),
            scratch_shapes=[total] * 4 + [ends] * 2 if backward else [],
        ),
        out_shape=[result] * (3 if backward else 1),
        compiler_params=pltpu.CompilerParams(vmem_limit_bytes=VMEM_LIMIT),
    )(
        random_rows.reshape(local_heads, -1),
        index,
        *operands,
        *([grads] if backward else []),
    )


def norm_forward(values, norm_gain, norm_shift):
    center = jnp.mean(values, axis=1, keepdims=True)
    spread = values - center
    variance = jnp.mean(spread * spread, axis=1, keepdims=True)
    inverse = lax.rsqrt(variance + EPS_NORM)
    normal = spread * inverse
    return ((normal * norm_gain + norm_shift).astype(BF16), normal, inverse)


def norm_backward(grad_norm, norm_gain, normal, inverse):
    scaled = grad_norm * norm_gain
    mean_plain = jnp.mean(scaled, axis=1, keepdims=True)
    mean_normal = jnp.mean(scaled * normal, axis=1, keepdims=True)
    grad_values = inverse * (scaled - mean_plain - normal * mean_normal)
    return (grad_values, jnp.sum(grad_norm * normal, axis=0), jnp.sum(grad_norm, axis=0))


def gelu_parts(values):
    square = values * values
    curve = jnp.tanh(GELU_SCALE * values * (1.0 + GELU_CUBE * square))
    half = 0.5 * (1.0 + curve)
    slope = half + 0.5 * values * (1.0 - curve * curve) * (
        GELU_SCALE * (1.0 + 3.0 * GELU_CUBE * square)
    )
    return values * half, slope


def rows_of(arrays, first, count):
    return jnp.concatenate([a[first : first + count] for a in arrays], axis=0)


def body(
    dp_size,
    mp_size,
    tokens,
    cotangent,
    w_qkv,
    w_out,
    w_up,
    w_down,
    gain_attn,
    shift_attn,
    gain_ffn,
    shift_ffn,
    bias_up,
    bias_down,
    random_blocks,
):
    paired = mp_size == 4
    outer = mp_size // 2
    index = lax.axis_index("mp").astype(jnp.int32).reshape(1)
    model = w_qkv.shape[1] * dp_size
    shard = w_qkv.shape[1]
    hidden = w_up.shape[1]
    attn = w_out.shape[0]
    lines = [[core + 2 * n for n in range(outer)] for core in range(2)]

    def to_low(value):
        return value.astype(BF16)

    qkv_low = lax.all_gather(
        to_low(w_qkv).transpose(1, 0, 2).reshape(shard, 3 * attn), "dp", axis=0, tiled=True
    )
    rest_low = lax.all_gather(
        jnp.concatenate([to_low(w_up), to_low(w_out).T, to_low(w_down).T], axis=1),
        "dp",
        axis=0,
        tiled=True,
    )
    up_low = rest_low[:, :hidden]
    out_low = rest_low[:, hidden : hidden + attn]
    down_low = rest_low[:, hidden + attn :]

    inputs = tokens[0].astype(F32)
    own_rows = inputs.shape[0]
    normed_low, normal_one, inverse_one = norm_forward(inputs, gain_attn, shift_attn)
    normed_full = jnp.concatenate(gather_pieces(normed_low, mp_size), axis=0)
    seq_rows = normed_full.shape[0]
    pieces = mp_size if paired else 1
    project = dot(normed_full, qkv_low, NN).astype(BF16)
    [heads_out] = attention_call(
        forward_kernel, 5, project, None, random_blocks[0], index, pieces
    )

    if paired:
        near_rows_count = seq_rows // 2
        outs = [heads_out[:near_rows_count], swap(heads_out[near_rows_count:], 2, mp_size)]
        out_parts = [out_low, swap(out_low, 2, mp_size)]
    else:
        moved = lax.all_to_all(
            heads_out, "mp", 0, 1, axis_index_groups=lines, tiled=True
        )
        outs = [moved]
        out_parts = [lax.all_gather(out_low, "mp", axis=1, axis_index_groups=lines, tiled=True)]
        core = lax.axis_index("mp") % 2

    def pair_order(value):
        if paired:
            return value
        half = value.shape[0] // 2
        return jnp.where(core == 0, value, jnp.roll(value, half, axis=0))

    outs = [pair_order(o) for o in outs]
    branch_pair = sum(dot(o, w, NT) for o, w in zip(outs, out_parts))
    branch = branch_pair[:own_rows] + swap(
        branch_pair[own_rows:].astype(BF16), 1, mp_size
    ).astype(F32)
    middle = inputs + branch
    second_low, normal_two, inverse_two = norm_forward(middle, gain_ffn, shift_ffn)
    second_full = jnp.concatenate(gather_pieces(second_low, mp_size), axis=0)
    grad_top = cotangent[0]
    grad_top_full = jnp.concatenate(gather_pieces(grad_top, mp_size), axis=0)
    active, slope = gelu_parts(dot(second_full, up_low, NN) + bias_up)
    active_low = active.astype(BF16)
    grad_hidden = (dot(grad_top_full, down_low, NN) * slope).astype(BF16)
    grad_second = scatter_sum(dot(grad_hidden, up_low, NT), mp_size)
    grad_bias_up = jnp.sum(grad_hidden.astype(F32), axis=0)
    grad_up_w = dot(second_full, grad_hidden, TN)
    grad_down_w = dot(grad_top_full, active_low, TN)

    grad_middle_norm, grad_gain_ffn, grad_shift_ffn = norm_backward(
        grad_second, gain_ffn, normal_two, inverse_two
    )
    grad_top_float = grad_top.astype(F32)
    grad_middle = grad_top_float + grad_middle_norm
    grad_bias_down = jnp.sum(grad_top_float, axis=0)
    grad_branch = grad_middle.astype(BF16)
    grad_pair = jnp.concatenate([grad_branch, swap(grad_branch, 1, mp_size)], axis=0)
    if paired:
        grad_heads = jnp.concatenate(
            [
                dot(grad_pair, out_parts[0], NN).astype(BF16),
                swap(dot(grad_pair, out_parts[1], NN).astype(BF16), 2, mp_size),
            ],
            axis=0,
        )
    else:
        moved = pair_order(dot(grad_pair, out_parts[0], NN).astype(BF16))
        grad_heads = lax.all_to_all(moved, "mp", 1, 0, axis_index_groups=lines, tiled=True)
    dq, dk, dv = attention_call(
        backward_kernel, 3, project, grad_heads, random_blocks[0], index, pieces
    )
    grad_project = jnp.concatenate([dq, dk, dv], axis=1)
    grad_qkv_w = dot(normed_full, grad_project, TN)
    grad_out_parts = [dot(grad_pair, o, TN).astype(BF16) for o in outs]
    if paired:
        grad_out_w = (
            grad_out_parts[0].astype(F32) + swap(grad_out_parts[1], 2, mp_size).astype(F32)
        ).astype(BF16)
    else:
        grad_out_w = lax.psum_scatter(
            grad_out_parts[0], "mp", scatter_dimension=1, axis_index_groups=lines, tiled=True
        )

    ffn_out = scatter_sum(dot(active_low, down_low, NT), mp_size)
    out_tokens = (middle + ffn_out + bias_down).astype(BF16)

    grad_normed = scatter_sum(dot(grad_project, qkv_low, NT), mp_size)
    grad_input_norm, grad_gain_attn, grad_shift_attn = norm_backward(
        grad_normed, gain_attn, normal_one, inverse_one
    )
    grad_tokens = (grad_middle + grad_input_norm)[None]

    def shard_sum(value):
        return lax.psum_scatter(
            value.astype(BF16), "dp", scatter_dimension=0, tiled=True
        ).astype(F32)

    ffn_shard = shard_sum(jnp.concatenate([grad_up_w.astype(BF16), grad_down_w.astype(BF16)], axis=1))
    attn_shard = shard_sum(jnp.concatenate([grad_qkv_w.astype(BF16), grad_out_w], axis=1))
    shards = [attn_shard[:, n * attn : (n + 1) * attn] for n in range(4)] + [
        ffn_shard[:, :hidden],
        ffn_shard[:, hidden:],
    ]
    squares = [g * g for g in shards]
    token_grads = [grad_gain_attn, grad_shift_attn, grad_gain_ffn, grad_shift_ffn, grad_bias_down]
    mp_sums = butterfly(
        jnp.concatenate([jnp.sum(s, axis=1) for s in squares] + token_grads), "mp", mp_size
    )
    model_sums = [mp_sums[n * shard : (n + 1) * shard] for n in range(6)]
    totals = jnp.stack([jnp.sum(s) for s in model_sums])
    local_sums = [jnp.sum(s, axis=0) for s in squares]
    dp_sums = butterfly(
        jnp.concatenate(
            local_sums
            + [mp_sums[6 * shard :], grad_bias_up, jnp.pad(totals, (0, 128 - totals.shape[0]))]
        ),
        "dp",
        dp_size,
    )
    cuts = []
    start = 0
    for length in [attn] * 4 + [hidden] * 2 + [model] * 5 + [hidden, 6]:
        cuts.append(dp_sums[start : start + length])
        start += length
    totals = cuts[12]

    def factored(gradient, model_sum, other_sum, whole_sum, other_total):
        model_mean = model_sum / other_total + EPS_FACTOR
        other_mean = other_sum / model + EPS_FACTOR
        whole = whole_sum / (model * other_total) + EPS_FACTOR
        model_factor = model_mean / whole
        other_factor = other_mean / whole
        update = gradient * lax.rsqrt(model_factor[:, None] * other_factor[None, :] * whole)
        return (LEARN_RATE * update, model_factor, other_factor)

    attn_total = attn * mp_size
    hidden_total = hidden * mp_size
    wide = [attn_total] * 4 + [hidden_total] * 2
    steps = [
        factored(shards[n], model_sums[n], cuts[n], totals[n], wide[n]) for n in range(6)
    ]
    new_qkv = w_qkv - jnp.stack([steps[n][0] for n in range(3)])
    return (
        out_tokens[None],
        grad_tokens,
        new_qkv,
        jnp.stack([steps[n][1] for n in range(3)]),
        jnp.stack([steps[n][2] for n in range(3)]),
        w_out - steps[3][0].T,
        steps[3][2],
        steps[3][1],
        w_up - steps[4][0],
        steps[4][1],
        steps[4][2],
        w_down - steps[5][0].T,
        steps[5][2],
        steps[5][1],
        cuts[6],
        cuts[7],
        cuts[8],
        cuts[9],
        cuts[11],
        cuts[10],
    )


def solution(mesh):
    placed = (
        P("dp", "mp", None),
        P("dp", "mp", None),
        P(None, "dp", "mp"),
        P("mp", "dp"),
        P("dp", "mp"),
        P("mp", "dp"),
        P(),
        P(),
        P(),
        P(),
        P("mp"),
        P(),
        P("dp", "mp", None, None),
    )
    return jax.shard_map(
        functools.partial(body, mesh.shape["dp"], mesh.shape["mp"]),
        mesh=mesh,
        in_specs=placed,
        out_specs=(
            P("dp", "mp", None),
            P("dp", "mp", None),
            P(None, "dp", "mp"),
            P(None, "dp"),
            P(None, "mp"),
            P("mp", "dp"),
            P("mp"),
            P("dp"),
            P("dp", "mp"),
            P("dp"),
            P("mp"),
            P("mp", "dp"),
            P("mp"),
            P("dp"),
            P(),
            P(),
            P(),
            P(),
            P("mp"),
            P(),
        ),
        check_vma=False,
    )
```

time: 1220 us -> 542 us (0.44)
  other arithmetic: 303 us -> 43.8 us
  local copies, waits for them, and re-layouts: 189 us -> 29.6 us
  waiting for transfers between devices: 397 us -> 267 us
  blocking collectives: 121 us -> 0 us
  matrix products: 175 us -> 94.9 us
  Pallas kernels: 0 us -> 61.7 us
  starting transfers between devices: 1.31 us -> 20.7 us
    scatter-add x8 -> x0, other arithmetic: 199 us -> none  [the longest x4 99.6 us: head_backward(): jax.ops.segment_sum(mid_value.reshape(-1, BLOCK, head_dim), segment_ids,...]
    ppermute x0 -> x26, waiting for transfers between devices: none -> 173 us  [swap(): return lax.ppermute(value, axis, [(i, i ^ bit) for i in range(size)])]
    all_gather x7 -> x2, waiting for transfers between devices: 219 us -> 66.2 us  [the longest x1 51.7 us: body(): lax.all_gather(jnp.concatenate([to_low(w_up), to_low(w_out).T, to_low(w_d...]
    psum x3 -> x0, blocking collectives: 89.7 us -> none  [the longest x1 40.4 us: body(): lax.psum((local_totals[0], local_totals[1], local_totals[2], local_totals...]
    reduce_scatter x5 -> x0, waiting for transfers between devices: 87.3 us -> none  [the longest x2 44.4 us: combine_grads(): lax.psum_scatter(partial_value.astype(jnp.bfloat16), 'mp', scatter_dimens...]
    unnamed x18 -> x6, waiting for transfers between devices: 90.8 us -> 27.5 us
    pallas_call x0 -> x2, Pallas kernels: none -> 61.7 us  [attention_call(): pl.pallas_call(functools.partial(kernel, width // head_dim, head_dim, dra...]
    dot_general x64 -> x15, matrix products: 156 us -> 94.9 us  [dot(): return lax.dot_general(left, right, form, preferred_element_type=F32)]
  transfers between devices with their start and end apart: 15 -> 30, of which waited for: 11 -> 19; matrix products, arithmetic and copies ran while one was open for 42% -> 26% of each run, Pallas kernels for 0% -> 11%
where the time goes in v1:
time: 542 us; the launch traced here: 536 us
  waiting for transfers between devices  267 us (49%)
  matrix products  94.9 us (18%)
  Pallas kernels  61.7 us (11%)
  other arithmetic  43.8 us (8%)
  local copies, waits for them, and re-layouts  29.6 us (5%)
  starting transfers between devices  20.7 us (4%)
  between operations  19.2 us (4%)
    ppermute x26, waiting for transfers between devices, swap(): return lax.ppermute(value, axis, [(i, i ^ bit) for i in range(size)])  173 us
    dot_general x15, matrix products, dot(): return lax.dot_general(left, right, form, preferred_element_type=F32)  94.9 us
    pallas_call x2, Pallas kernels, attention_call(): pl.pallas_call(functools.partial(kernel, width // head_dim, head_dim, dra...  61.7 us
    all_gather x1, waiting for transfers between devices, body(): lax.all_gather(jnp.concatenate([to_low(w_up), to_low(w_out).T, to_low(w_d...  51.7 us
    unnamed x6, waiting for transfers between devices  27.5 us
    unnamed x135, local copies, waits for them, and re-layouts  22.3 us
    ppermute x26, starting transfers between devices, swap(): return lax.ppermute(value, axis, [(i, i ^ bit) for i in range(size)])  20.5 us
    all_gather x1, waiting for transfers between devices, body(): lax.all_gather(to_low(w_qkv).transpose(1, 0, 2).reshape(shard, 3 * attn),...  14.5 us
  transfers between devices with their start and end apart: 30, of which 19 were waited for; matrix products, arithmetic and copies ran while one was open for 26% of the time, Pallas kernels for 11%

profile of v1, /device:TPU:0, one launch (start us, length us, event | category | flops | bytes accessed | tf_op | source)
XLA Modules:
  0.0 536.4 jit_solution(15107135778885292569)
XLA Ops:
  14.9 3.0 collective-permute-start.1
  17.9 23.3 %collective-permute-done.1 = bf16[512,1024]{1,0:T(8,128)(2,1)} collective-permute-done((bf16[512,1024]{1,0:T(8,128)(2,1)S(1)}, bf16[512,1024]{1,0:T(8,128)(2,1)}, u32[]{:S(2)}, u32[]{:S(2)}) %collective-permute-start.1) | collective-permute-done | bytes 1048608 | tf_op jit(solution)/shard_map/ppermute | solution.py:30
  41.5 2.7 collective-permute-done.2
  44.2 14.5 %all-gather.3.cloned.1.call-done = bf16[1024,768]{0,1:T(8,128)(2,1)} async-done(((bf16[128,768]{0,1:T(8,128)(2,1)}), bf16[1024,768]{0,1:T(8,128)(2,1)}) %all-gather.3.cloned.1.call-update) | async-done | bytes 1572880 | tf_op jit(solution)/shard_map/all_gather | solution.py:337
  58.7 6.2 %convolution_convert_fusion.q_ref.k_ref.v_ref = bf16[2048,768]{1,0:T(8,128)(2,1)S(1)} fusion(bf16[1024,768]{0,1:T(8,128)(2,1)} %all-gather.3.cloned.1.call-done, bf16[512,1024]{1,0:T(8,128)(2,1)} %collective-permute-done.2, bf16[512,1024]{1,0:T(8,128)(2,1)} %collective-permute-done.1, bf16[512,1024]{1,0:T(8,128)(2,1)} %collective-permute-done, ...), kind=kOutput, calls=%fused_computation.9 | convolution fusion | flops 3239575552 | bytes 8912896 | tf_op jit(solution)/shard_map/dot_general | solution.py:26
  64.9 20.7 %shard_map.284 = bf16[2048,256]{1,0:T(8,128)(2,1)S(1)} custom-call(s32[4,90]{1,0:T(4,128)S(1)} %reshape_squeeze.4.random_ref, s32[1]{0:T(128)} %bitcast.1.index_ref, bf16[2048,768]{1,0:T(8,128)(2,1)S(1)} %convolution_convert_fusion.q_ref.k_ref.v_ref, bf16[2048,768]{1,0:T(8,128)(2,1)S(1)} %convolution_convert_fusion.q_ref.k_ref.v_ref, ...), custom_call_target="tpu_custom_call" | custom-call | tf_op jit(solution)/shard_map/pallas_call | solution.py:258
  88.9 51.7 %all-gather.5.cloned.1.call-done = bf16[1024,2304]{0,1:T(8,128)(2,1)} async-done(((bf16[128,2304]{0,1:T(8,128)(2,1)}), bf16[1024,2304]{0,1:T(8,128)(2,1)}) %all-gather.5.cloned.1.call-update) | async-done | bytes 4718608 | tf_op jit(solution)/shard_map/all_gather | solution.py:340
  143.3 1.9 fusion.42
  145.2 9.8 %collective-permute-done.4 = bf16[1024,256]{0,1:T(8,128)(2,1)S(1)} collective-permute-done((bf16[1024,256]{0,1:T(8,128)(2,1)S(1)}, bf16[1024,256]{0,1:T(8,128)(2,1)S(1)}, u32[]{:S(2)}, u32[]{:S(2)}) %collective-permute-start.4) | collective-permute-done | bytes 524320 | tf_op jit(solution)/shard_map/ppermute | solution.py:30
  155.0 2.0 convolution_add_fusion
  157.3 2.6 collective-permute-done.5
  164.2 24.0 %collective-permute-done.7 = bf16[512,1024]{1,0:T(8,128)(2,1)S(1)} collective-permute-done((bf16[512,1024]{1,0:T(8,128)(2,1)S(1)}, bf16[512,1024]{1,0:T(8,128)(2,1)S(1)}, u32[]{:S(2)}, u32[]{:S(2)}) %collective-permute-start.7) | collective-permute-done | bytes 1048608 | tf_op jit(solution)/shard_map/ppermute | solution.py:30
  188.7 21.2 %collective-permute-done.12 = bf16[512,1024]{1,0:T(8,128)(2,1)S(1)} collective-permute-done((bf16[512,1024]{1,0:T(8,128)(2,1)S(1)}, bf16[512,1024]{1,0:T(8,128)(2,1)S(1)}, u32[]{:S(2)}, u32[]{:S(2)}) %collective-permute-start.12) | collective-permute-done | bytes 1048608 | tf_op jit(solution)/shard_map/ppermute | solution.py:30
  209.9 11.0 %fusion.31 = f32[2048,1024]{1,0:T(8,128)} fusion(bf16[1024,2304]{0,1:T(8,128)(2,1)S(1)} %bitcast.99, bf16[512,1024]{1,0:T(8,128)(2,1)S(1)} %collective-permute-done.8, bf16[512,1024]{1,0:T(8,128)(2,1)S(1)} %collective-permute-done.7, bf16[512,1024]{1,0:T(8,128)(2,1)S(1)} %collective-permute-done.6, bf16[512,1024]{1,0:T(8,128)(2,1)S(1)} %add_convert_fusion), kind=kOutput, calls=%fused_computation.66 | convolution fusion | flops 4311744512 | bytes 14680064 | tf_op jit(solution)/shard_map/dot_general | solution.py:26
  220.9 12.3 %fusion.83 = (bf16[2048,1024]{1,0:T(8,128)(2,1)S(1)}, f32[2048,1024]{1,0:T(8,128)}) fusion(bf16[1024,2304]{0,1:T(8,128)(2,1)S(1)} %bitcast.99, f32[2048,1024]{1,0:T(8,128)} %fusion.31, f32[1024]{0:T(1024)S(1)} %copy-done.49), kind=kOutput, calls=%fused_computation.190 | convolution fusion | flops 4318035968 | bytes 23072768 | tf_op jit(solution)/shard_map/dot_general | solution.py:26
  235.4 18.5 %convert_reduce_fusion = (f32[1024]{0:T(1024)S(1)}, bf16[2048,1024]{1,0:T(8,128)(2,1)}) fusion(f32[2048,1024]{1,0:T(8,128)} %fusion.31, f32[1024]{0:T(1024)S(1)} %copy-done.49, bf16[1024,2304]{0,1:T(8,128)(2,1)S(1)} %bitcast.99, bf16[512,1024]{1,0:T(8,128)(2,1)S(1)} %collective-permute-done.13, bf16[512,1024]{1,0:T(8,128)(2,1)S(1)} %collective-permute-done.12, ...), kind=kOutput, calls=%fused_computation | convolution fusion | flops 4355783680 | bytes 18882560 | tf_op jit(solution)/shard_map/dot_general | solution.py:26
  253.9 9.1 %fusion.82 = (bf16[2048,1024]{1,0:T(8,128)(2,1)S(1)}, f32[2048,1024]{1,0:T(8,128)}) fusion(bf16[2048,1024]{1,0:T(8,128)(2,1)} %get-tuple-element.160, bf16[1024,2304]{0,1:T(8,128)(2,1)S(1)} %bitcast.99), kind=kOutput, calls=%fused_computation.189 | convolution fusion | flops 4297064448 | bytes 18874368 | tf_op jit(solution)/shard_map/dot_general | solution.py:26
  265.6 9.7 %convolution_convert_fusion.1 = bf16[1024,1024]{0,1:T(8,128)(2,1)S(1)} fusion(bf16[512,1024]{1,0:T(8,128)(2,1)S(1)} %copy-done.48, bf16[512,1024]{1,0:T(8,128)(2,1)S(1)} %copy-done.42, bf16[512,1024]{1,0:T(8,128)(2,1)S(1)} %copy-done.46, bf16[512,1024]{1,0:T(8,128)(2,1)S(1)} %bitcast.96, f32[2048,1024]{1,0:T(8,128)} %fusion.31, f32[1024]{0:T(1024)S(1)} %copy-done.49), kind=kOutput, calls=%fused_computation.59 | convolution fusion | flops 4333764608 | bytes 14684160 | tf_op jit(solution)/shard_map/dot_general | solution.py:26
  275.3 4.8 convolution_convert_fusion.2
  280.1 2.4 pad_maximum_fusion.3
  282.5 6.5 %copy.59 = bf16[1024,2048]{1,0:T(8,128)(2,1)} copy(bf16[1024,2048]{0,1:T(8,128)(2,1)} %pad_maximum_fusion.3) | data formatting | bytes 8388608
  289.2 2.4 fusion.19
  293.1 2.2 fusion.21
  295.9 21.7 %collective-permute-done.15 = bf16[512,1024]{1,0:T(8,128)(2,1)S(1)} collective-permute-done((bf16[512,1024]{1,0:T(8,128)(2,1)S(1)}, bf16[512,1024]{1,0:T(8,128)(2,1)S(1)}, u32[]{:S(2)}, u32[]{:S(2)}) %collective-permute-start.15) | collective-permute-done | bytes 1048608 | tf_op jit(solution)/shard_map/ppermute | solution.py:30
  317.6 3.0 multiply_reduce_fusion
  320.6 18.5 %collective-permute-done.10 = bf16[512,1024]{1,0:T(8,128)(2,1)S(1)} collective-permute-done((bf16[512,1024]{1,0:T(8,128)(2,1)S(1)}, bf16[512,1024]{1,0:T(8,128)(2,1)S(1)}, u32[]{:S(2)}, u32[]{:S(2)}) %collective-permute-start.10) | collective-permute-done | bytes 1048608 | tf_op jit(solution)/shard_map/ppermute | solution.py:30
  339.2 4.1 fusion.73
  343.3 2.7 collective-permute-done.16
  348.3 1.8 convolution_convert_fusion.4
  350.7 1.8 convolution_convert_fusion.7
  352.5 9.1 %collective-permute-done.17 = bf16[1024,256]{1,0:T(8,128)(2,1)S(1)} collective-permute-done((bf16[1024,256]{1,0:T(8,128)(2,1)S(1)}, bf16[1024,256]{1,0:T(8,128)(2,1)S(1)}, u32[]{:S(2)}, u32[]{:S(2)}) %collective-permute-start.17) | collective-permute-done | bytes 524320 | tf_op jit(solution)/shard_map/ppermute | solution.py:30
  361.6 41.0 %shard_map.285 = (bf16[2048,256]{1,0:T(8,128)(2,1)S(1)}, bf16[2048,256]{1,0:T(8,128)(2,1)S(1)}, bf16[2048,256]{1,0:T(8,128)(2,1)S(1)}) custom-call(s32[4,90]{1,0:T(4,128)S(1)} %reshape_squeeze.4.random_ref, s32[1]{0:T(128)} %bitcast.1.index_ref, bf16[2048,768]{1,0:T(8,128)(2,1)S(1)} %convolution_convert_fusion.q_ref.k_ref.v_ref, ...), custom_call_target="tpu_custom_call" | custom-call | tf_op jit(solution)/shard_map/pallas_call | solution.py:258
  405.1 5.4 %convolution_convert_fusion.3 = bf16[1024,768]{0,1:T(8,128)(2,1)S(1)} fusion(bf16[2048,768]{1,0:T(8,128)(2,1)S(1)} %constant_dynamic-update-slice_fusion, bf16[512,1024]{1,0:T(8,128)(2,1)} %collective-permute-done.2, bf16[512,1024]{1,0:T(8,128)(2,1)} %collective-permute-done.1, bf16[512,1024]{1,0:T(8,128)(2,1)} %collective-permute-done, ...), kind=kOutput, calls=%fused_computation.70 | convolution fusion | flops 3238789120 | bytes 8912896 | tf_op jit(solution)/shard_map/dot_general | solution.py:26
  410.6 2.8 copy.57
  413.5 9.0 %fusion.84 = (bf16[2048,1024]{1,0:T(8,128)(2,1)S(1)}, f32[2048,1024]{1,0:T(8,128)}) fusion(bf16[2048,768]{1,0:T(8,128)(2,1)} %copy-done.19, bf16[1024,768]{0,1:T(8,128)(2,1)} %all-gather.3.cloned.1.call-done), kind=kOutput, calls=%fused_computation.191 | convolution fusion | flops 3223322624 | bytes 17301504 | tf_op jit(solution)/shard_map/dot_general | solution.py:26
  423.0 4.1 collective-permute-done.18
  428.4 2.0 fusion.17
  430.5 1.7 collective-permute-start.19
  432.1 23.6 %collective-permute-done.19 = bf16[512,1024]{1,0:T(8,128)(2,1)S(1)} collective-permute-done((bf16[512,1024]{1,0:T(8,128)(2,1)S(1)}, bf16[512,1024]{1,0:T(8,128)(2,1)S(1)}, u32[]{:S(2)}, u32[]{:S(2)}) %collective-permute-start.19) | collective-permute-done | bytes 1048608 | tf_op jit(solution)/shard_map/ppermute | solution.py:30
  455.8 4.2 fusion.15
  461.7 27.4 %reduce-scatter.7.cloned.1.call-done = bf16[128,1024]{1,0:T(8,128)(2,1)} async-done(((bf16[1024,1024]{1,0:T(8,128)(2,1)}), bf16[128,1024]{1,0:T(8,128)(2,1)}) %reduce-scatter.7.cloned.1.call-update) | async-done | bytes 262160
  493.5 2.3 collective-permute-done.22
  496.4 4.0 stack.57
  501.2 3.2 collective-permute-done.23
  505.4 3.1 collective-permute-done.24
  508.4 1.8 collective-permute-start.25
  510.2 4.3 fusion.14
  526.5 1.7 bitcast_subtract_fusion.1
  (234 shorter events, 50.7 us)
Async XLA Ops:
  7.2 51.5 %all-gather.3.cloned.1.call-start = ((), (), s32[]{:S(2)}) async-start(), calls=%async_computation.2 | async-start | bytes 1769472 | tf_op jit(solution)/shard_map/all_gather | solution.py:337
  9.3 31.9 %copy-start.31 = (s32[1,4,30,3]{2,1,3,0:T(4,128)S(1)}, s32[1,4,30,3]{2,1,3,0:T(4,128)}, u32[]{:S(2)}) copy-start(s32[1,4,30,3]{2,1,3,0:T(4,128)} %param.25) | copy-start | bytes 4324
  9.3 131.3 %all-gather.5.cloned.1.call-start = ((), (), s32[]{:S(2)}) async-start(), calls=%async_computation.3 | async-start | bytes 5308416 | tf_op jit(solution)/shard_map/all_gather | solution.py:340
  10.6 33.6 %copy-start.7 = (f32[128,1024]{0,1:T(8,128)}, f32[128,1024]{0,1:T(8,128)S(1)}, u32[]{:S(2)}) copy-start(f32[128,1024]{0,1:T(8,128)S(1)} %copy.50) | copy-start | bytes 1572868
  13.7 446.3 %reduce-scatter.9.cloned.1.call-start = ((), (), s32[]{:S(2)}) async-start(), calls=%async_computation.5 | async-start | bytes 4718592
  14.0 27.2 %copy-start.21 = (f32[512]{0:T(512)}, f32[512]{0:T(512)S(1)}, u32[]{:S(2)}) copy-start(f32[512]{0:T(512)S(1)} %broadcast_multiply_fusion.5) | copy-start | bytes 6148
  14.4 26.8 %copy-start.26 = (f32[512]{0:T(512)}, f32[512]{0:T(512)S(1)}, u32[]{:S(2)}) copy-start(f32[512]{0:T(512)S(1)} %add_rsqrt_fusion.1) | copy-start | bytes 6148
  14.9 29.3 %copy-start.15 = (bf16[512,1024]{1,0:T(8,128)(2,1)}, bf16[512,1024]{1,0:T(8,128)(2,1)S(1)}, u32[]{:S(2)}) copy-start(bf16[512,1024]{1,0:T(8,128)(2,1)S(1)} %fusion.9) | copy-start | bytes 3145732
  14.9 26.3 %collective-permute-start.1 = (bf16[512,1024]{1,0:T(8,128)(2,1)S(1)}, bf16[512,1024]{1,0:T(8,128)(2,1)}, u32[]{:S(2)}, u32[]{:S(2)}) collective-permute-start(bf16[512,1024]{1,0:T(8,128)(2,1)S(1)} %fusion.9), channel_id=1, source_target_pairs={{0,2},{1,3},{2,0},{3,1},{4,6},{5,7},{6,4},{7,5},{8,10},{9,11},{10,... | collective-permute-start | bytes 3145736 | tf_op jit(solution)/shard_map/ppermute | solution.py:30
  17.9 23.5 %collective-permute-start = (bf16[512,1024]{1,0:T(8,128)(2,1)S(1)}, bf16[512,1024]{1,0:T(8,128)(2,1)}, u32[]{:S(2)}, u32[]{:S(2)}) collective-permute-start(bf16[512,1024]{1,0:T(8,128)(2,1)S(1)} %fusion.9), channel_id=1, source_target_pairs={{0,1},{1,0},{2,3},{3,2},{4,5},{5,4},{6,7},{7,6},{8,9},{9,8},{10,11... | collective-permute-start | bytes 3145736 | tf_op jit(solution)/shard_map/ppermute | solution.py:30
  41.2 3.0 collective-permute-start.2
  87.4 57.8 %collective-permute-start.3 = (bf16[1024,256]{1,0:T(8,128)(2,1)}, bf16[1024,256]{1,0:T(8,128)(2,1)}, u32[]{:S(2)}, u32[]{:S(2)}) collective-permute-start(bf16[1024,256]{1,0:T(8,128)(2,1)} %slice.234), channel_id=1, source_target_pairs={{0,2},{1,3},{2,0},{3,1},{4,6},{5,7},{6,4},{7,5},{8,10},{9,11},{10,... | collective-permute-start | bytes 1572872 | tf_op jit(solution)/shard_map/ppermute | solution.py:30
  141.7 13.3 %collective-permute-start.4 = (bf16[1024,256]{0,1:T(8,128)(2,1)S(1)}, bf16[1024,256]{0,1:T(8,128)(2,1)S(1)}, u32[]{:S(2)}, u32[]{:S(2)}) collective-permute-start(bf16[1024,256]{0,1:T(8,128)(2,1)S(1)} %slice.233), channel_id=1, source_target_pairs={{0,2},{1,3},{2,0},{3,1},{4,6},{5,7},{6,4},{7,5},{8,10},{9,11},{10,... | collective-permute-start | bytes 1572872 | tf_op jit(solution)/shard_map/ppermute | solution.py:30
  157.0 52.8 %slice-start = ((s8[4718592]{0:T(1024)(128)(4,1)}), s8[4194304]{0:T(1024)(128)(4,1)S(1)}, s32[]{:S(2)}) async-start(s8[4718592]{0:T(1024)(128)(4,1)} %bitcast.98), calls=%async_computation.6 | async-start | bytes 8388608
  157.2 52.7 %slice-start.1 = ((s8[4718592]{0:T(1024)(128)(4,1)}), s8[524288]{0:T(1024)(128)(4,1)S(1)}, s32[]{:S(2)}) async-start(s8[4718592]{0:T(1024)(128)(4,1)} %bitcast.98), calls=%async_computation.7 | async-start | bytes 1048576
  157.2 2.7 collective-permute-start.5
  162.1 26.1 %collective-permute-start.7 = (bf16[512,1024]{1,0:T(8,128)(2,1)S(1)}, bf16[512,1024]{1,0:T(8,128)(2,1)S(1)}, u32[]{:S(2)}, u32[]{:S(2)}) collective-permute-start(bf16[512,1024]{1,0:T(8,128)(2,1)S(1)} %add_convert_fusion), channel_id=1, source_target_pairs={{0,2},{1,3},{2,0},{3,1},{4,6},{5,7},{6,4},{7,5},{8,10},{9,11},{10,... | collective-permute-start | bytes 3145736 | tf_op jit(solution)/shard_map/ppermute | solution.py:30
  163.7 57.2 %copy-start.49 = (f32[1024]{0:T(1024)S(1)}, f32[1024]{0:T(1024)}, u32[]{:S(2)}) copy-start(f32[1024]{0:T(1024)} %param.23) | copy-start | bytes 12292
  163.7 46.1 %collective-permute-start.12 = (bf16[512,1024]{1,0:T(8,128)(2,1)S(1)}, bf16[512,1024]{1,0:T(8,128)(2,1)S(1)}, u32[]{:S(2)}, u32[]{:S(2)}) collective-permute-start(bf16[512,1024]{1,0:T(8,128)(2,1)S(1)} %bitcast.93), channel_id=1, source_target_pairs={{0,2},{1,3},{2,0},{3,1},{4,6},{5,7},{6,4},{7,5},{8,10},{9,11},{10,... | collective-permute-start | bytes 3145736 | tf_op jit(solution)/shard_map/ppermute | solution.py:30
  164.2 45.6 %collective-permute-start.6 = (bf16[512,1024]{1,0:T(8,128)(2,1)S(1)}, bf16[512,1024]{1,0:T(8,128)(2,1)S(1)}, u32[]{:S(2)}, u32[]{:S(2)}) collective-permute-start(bf16[512,1024]{1,0:T(8,128)(2,1)S(1)} %add_convert_fusion), channel_id=1, source_target_pairs={{0,1},{1,0},{2,3},{3,2},{4,5},{5,4},{6,7},{7,6},{8,9},{9,8},{10,11... | collective-permute-start | bytes 3145736 | tf_op jit(solution)/shard_map/ppermute | solution.py:30
  188.2 21.7 %collective-permute-start.8 = (bf16[512,1024]{1,0:T(8,128)(2,1)S(1)}, bf16[512,1024]{1,0:T(8,128)(2,1)S(1)}, u32[]{:S(2)}, u32[]{:S(2)}) collective-permute-start(bf16[512,1024]{1,0:T(8,128)(2,1)S(1)} %collective-permute-done.7), channel_id=1, source_target_pairs={{0,1},{1,0},{2,3},{3,2},{4,5},{5,4},{6,7},{7,6},{8,9},{9,8},{10,11... | collective-permute-start | bytes 3145736 | tf_op jit(solution)/shard_map/ppermute | solution.py:30
  188.2 47.2 %collective-permute-start.11 = (bf16[512,1024]{1,0:T(8,128)(2,1)S(1)}, bf16[512,1024]{1,0:T(8,128)(2,1)S(1)}, u32[]{:S(2)}, u32[]{:S(2)}) collective-permute-start(bf16[512,1024]{1,0:T(8,128)(2,1)S(1)} %bitcast.94), channel_id=1, source_target_pairs={{0,1},{1,0},{2,3},{3,2},{4,5},{5,4},{6,7},{7,6},{8,9},{9,8},{10,11... | collective-permute-start | bytes 3145736 | tf_op jit(solution)/shard_map/ppermute | solution.py:30
  209.9 25.6 %copy-start.41 = (bf16[512,1024]{1,0:T(8,128)(2,1)}, bf16[512,1024]{1,0:T(8,128)(2,1)S(1)}, u32[]{:S(2)}) copy-start(bf16[512,1024]{1,0:T(8,128)(2,1)S(1)} %collective-permute-done.12) | copy-start | bytes 3145732
  209.9 25.5 %collective-permute-start.13 = (bf16[512,1024]{1,0:T(8,128)(2,1)S(1)}, bf16[512,1024]{1,0:T(8,128)(2,1)S(1)}, u32[]{:S(2)}, u32[]{:S(2)}) collective-permute-start(bf16[512,1024]{1,0:T(8,128)(2,1)S(1)} %collective-permute-done.12), channel_id=1, source_target_pairs={{0,1},{1,0},{2,3},{3,2},{4,5},{5,4},{6,7},{7,6},{8,9},{9,8},{10,11... | collective-permute-start | bytes 3145736 | tf_op jit(solution)/shard_map/ppermute | solution.py:30
  234.9 58.2 %collective-permute-start.9 = (bf16[1024,1024]{1,0:T(8,128)(2,1)}, bf16[1024,1024]{1,0:T(8,128)(2,1)}, u32[]{:S(2)}, u32[]{:S(2)}) collective-permute-start(bf16[1024,1024]{1,0:T(8,128)(2,1)} %pad_maximum_fusion.4), channel_id=1, source_target_pairs={{0,1},{1,0},{2,3},{3,2},{4,5},{5,4},{6,7},{7,6},{8,9},{9,8},{10,11... | collective-permute-start | bytes 6291464 | tf_op jit(solution)/shard_map/ppermute | solution.py:30
  235.4 18.5 %copy-start.45 = (bf16[512,1024]{1,0:T(8,128)(2,1)}, bf16[512,1024]{1,0:T(8,128)(2,1)S(1)}, u32[]{:S(2)}) copy-start(bf16[512,1024]{1,0:T(8,128)(2,1)S(1)} %collective-permute-done.11) | copy-start | bytes 3145732
  264.7 24.4 %collective-permute-start.14 = (bf16[1024,1024]{1,0:T(8,128)(2,1)}, bf16[1024,1024]{1,0:T(8,128)(2,1)}, u32[]{:S(2)}, u32[]{:S(2)}) collective-permute-start(bf16[1024,1024]{1,0:T(8,128)(2,1)} %pad_maximum_fusion.5), channel_id=1, source_target_pairs={{0,1},{1,0},{2,3},{3,2},{4,5},{5,4},{6,7},{7,6},{8,9},{9,8},{10,11... | collective-permute-start | bytes 6291464 | tf_op jit(solution)/shard_map/ppermute | solution.py:30
  289.1 200.0 %reduce-scatter.7.cloned.1.call-start = ((), (), s32[]{:S(2)}) async-start(), calls=%async_computation.4 | async-start | bytes 2359296
  289.2 28.5 %copy-start.3 = (f32[512,1024]{1,0:T(8,128)S(1)}, f32[512,1024]{1,0:T(8,128)}, u32[]{:S(2)}) copy-start(f32[512,1024]{1,0:T(8,128)} %copy-done.2) | copy-start | bytes 6291460
  291.5 26.1 %collective-permute-start.15 = (bf16[512,1024]{1,0:T(8,128)(2,1)S(1)}, bf16[512,1024]{1,0:T(8,128)(2,1)S(1)}, u32[]{:S(2)}, u32[]{:S(2)}) collective-permute-start(bf16[512,1024]{1,0:T(8,128)(2,1)S(1)} %fusion.19), channel_id=1, source_target_pairs={{0,2},{1,3},{2,0},{3,1},{4,6},{5,7},{6,4},{7,5},{8,10},{9,11},{10,... | collective-permute-start | bytes 3145736 | tf_op jit(solution)/shard_map/ppermute | solution.py:30
  295.3 43.8 %copy-start.14 = (bf16[1,512,1024]{2,1,0:T(8,128)(2,1)S(1)}, bf16[1,512,1024]{2,1,0:T(8,128)(2,1)}, u32[]{:S(2)}) copy-start(bf16[1,512,1024]{2,1,0:T(8,128)(2,1)} %param.14) | copy-start | bytes 3145732
  295.3 43.8 %copy-start.35 = (f32[1024]{0:T(1024)S(1)}, f32[1024]{0:T(1024)}, u32[]{:S(2)}) copy-start(f32[1024]{0:T(1024)} %param.24) | copy-start | bytes 12292
  295.4 43.8 %collective-permute-start.10 = (bf16[512,1024]{1,0:T(8,128)(2,1)S(1)}, bf16[512,1024]{1,0:T(8,128)(2,1)S(1)}, u32[]{:S(2)}, u32[]{:S(2)}) collective-permute-start(bf16[512,1024]{1,0:T(8,128)(2,1)S(1)} %fusion.21), channel_id=1, source_target_pairs={{0,2},{1,3},{2,0},{3,1},{4,6},{5,7},{6,4},{7,5},{8,10},{9,11},{10,... | collective-permute-start | bytes 3145736 | tf_op jit(solution)/shard_map/ppermute | solution.py:30
  343.3 2.7 collective-permute-start.16
  346.7 14.8 %collective-permute-start.17 = (bf16[1024,256]{1,0:T(8,128)(2,1)S(1)}, bf16[1024,256]{1,0:T(8,128)(2,1)S(1)}, u32[]{:S(2)}, u32[]{:S(2)}) collective-permute-start(bf16[1024,256]{1,0:T(8,128)(2,1)S(1)} %convolution_convert_fusion.6), channel_id=1, source_target_pairs={{0,2},{1,3},{2,0},{3,1},{4,6},{5,7},{6,4},{7,5},{8,10},{9,11},{10,... | collective-permute-start | bytes 1572872 | tf_op jit(solution)/shard_map/ppermute | solution.py:30
  350.1 52.7 %collective-permute-start.20 = (bf16[1024,256]{0,1:T(8,128)(2,1)S(1)}, bf16[1024,256]{0,1:T(8,128)(2,1)S(1)}, u32[]{:S(2)}, u32[]{:S(2)}) collective-permute-start(bf16[1024,256]{0,1:T(8,128)(2,1)S(1)} %convolution_convert_fusion.4), channel_id=1, source_target_pairs={{0,2},{1,3},{2,0},{3,1},{4,6},{5,7},{6,4},{7,5},{8,10},{9,11},{10,... | collective-permute-start | bytes 1572872 | tf_op jit(solution)/shard_map/ppermute | solution.py:30
  422.7 33.1 %copy-start.6 = (bf16[1,512,1024]{2,1,0:T(8,128)(2,1)S(1)}, bf16[1,512,1024]{2,1,0:T(8,128)(2,1)}, u32[]{:S(2)}) copy-start(bf16[1,512,1024]{2,1,0:T(8,128)(2,1)} %param.13) | copy-start | bytes 3145732
  422.7 33.1 %copy-start.22 = (f32[512]{0:T(512)S(1)}, f32[512]{0:T(512)}, u32[]{:S(2)}) copy-start(f32[512]{0:T(512)} %copy-done.21) | copy-start | bytes 6148
  422.7 33.0 %copy-start.25 = (f32[1024]{0:T(1024)S(1)}, f32[1024]{0:T(1024)}, u32[]{:S(2)}) copy-start(f32[1024]{0:T(1024)} %param.19) | copy-start | bytes 12292
  422.7 33.0 %copy-start.27 = (f32[512]{0:T(512)S(1)}, f32[512]{0:T(512)}, u32[]{:S(2)}) copy-start(f32[512]{0:T(512)} %copy-done.26) | copy-start | bytes 6148
  422.9 4.2 collective-permute-start.18
  430.5 25.3 %collective-permute-start.19 = (bf16[512,1024]{1,0:T(8,128)(2,1)S(1)}, bf16[512,1024]{1,0:T(8,128)(2,1)S(1)}, u32[]{:S(2)}, u32[]{:S(2)}) collective-permute-start(bf16[512,1024]{1,0:T(8,128)(2,1)S(1)} %fusion.17), channel_id=1, source_target_pairs={{0,2},{1,3},{2,0},{3,1},{4,6},{5,7},{6,4},{7,5},{8,10},{9,11},{10,... | collective-permute-start | bytes 3145736 | tf_op jit(solution)/shard_map/ppermute | solution.py:30
  490.5 31.2 %copy-start.8 = (f32[128,1024]{0,1:T(8,128)S(1)}, f32[128,1024]{0,1:T(8,128)}, u32[]{:S(2)}) copy-start(f32[128,1024]{0,1:T(8,128)} %copy-done.7) | copy-start | bytes 1572868
  490.7 1.3 collective-permute-start.21
  491.9 3.8 collective-permute-start.22
  500.4 4.0 collective-permute-start.23
  504.4 4.0 collective-permute-start.24
  508.4 6.1 %collective-permute-start.25 = (f32[9344]{0:T(1024)S(1)}, f32[9344]{0:T(1024)S(1)}, u32[]{:S(2)}, u32[]{:S(2)}) collective-permute-start(f32[9344]{0:T(1024)S(1)} %add.235), channel_id=1, source_target_pairs={{0,16},{4,20},{8,24},{12,28},{16,0},{20,4},{24,8},{28,12},{1,17},{... | collective-permute-start | bytes 112136 | tf_op jit(solution)/shard_map/ppermute | solution.py:30
  (35 other events, 199.2 us)
Sparse Core Ops, SparseCore 0:
  10.7 47.9 all-gather.2
  61.3 79.2 all-gather.4
  289.2 86.7 reduce-scatter.8
  422.8 66.2 reduce-scatter.6
